TPU v7x, 512 devices: a whole 4x8x8 slice. The times are simulated.
512 devices in a mesh: depth: 16 (over x_hi, z), scan: 32 (over x_lo, y, core).
Axes of the slice: x: 4 (x_hi: 2, x_lo: 2; x = x_hi * 2 + x_lo), y: 8, z: 8, core: 2. Of those that a mesh axis runs over, the one named last changes fastest.
Arguments:
- object_slices: float32 [16, 2, 4096, 384], P('depth', None, 'scan'), may hold values from -1.25 to 1.25, as said below
- probe: float32 [2, 256, 256], replicated, may hold values from -4 to 4
- offsets: int32 [64, 2], P('scan'), may hold values from 0 to 128
- intensity: float32 [64, 256, 256], P('scan'), may hold values from 0.03 to 1
Outputs:
- object_grad: float32 [16, 2, 4096, 384], P('depth', None, 'scan')
- probe_grad: float32 [2, 256, 256], P(None, 'scan', 'depth')
Inputs may be any that keep to these rules, and one draw needn't show every extreme that they name: `offsets`: column 0 is a window's first row counted from 128 rows above the first object row of its scan index, wrapping around the object; column 1 is its first column. `object_slices`: real and imaginary parts of each slice's transmission.
All inputs are finite; a program needn't handle non-finite values.
Results may differ from a plain program's by a relative error of at most 0.035.
Values may be sent and summed in bfloat16 or wider, within the bound.
A program may use at most 64 MiB of HBM per device.

v0:
```python
import math

import jax
import jax.numpy as jnp
from jax import lax
from jax.sharding import PartitionSpec as P

HALO = 128


PHASE_SCALE = 16.0


def padded(cells, sides, width):
    for axis, dim in sides:
        count = lax.axis_size(axis)
        head = lax.slice_in_dim(cells, 0, width, axis=dim)
        tail = lax.slice_in_dim(cells, cells.shape[dim] - width, cells.shape[dim], axis=dim)
        cells = jnp.concatenate(
            [
                lax.ppermute(tail, axis, [(i, (i + 1) % count) for i in range(count)]),
                cells,
                lax.ppermute(head, axis, [((i + 1) % count, i) for i in range(count)]),
            ],
            axis=dim,
        )
    return cells


def from_behind(block, axis, distance):
    devices = range(lax.axis_size(axis))
    route = [(i - distance, i) for i in devices if i - distance in devices]
    return lax.ppermute(block, axis, route)


def passed_along(block, axis, distance):
    devices = range(lax.axis_size(axis))
    route = [((i - distance) % len(devices), i) for i in devices]
    return lax.ppermute(block, axis, route)


def dft_table(length, sign_value):
    places = jnp.arange(length, dtype=jnp.int32)
    product = places[:, None] * places[None, :] % length
    angles = product.astype(jnp.float32) * jnp.float32(2.0 * math.pi / length)
    factor = jnp.float32(1.0 / math.sqrt(length))
    cosine = jnp.cos(angles) * factor
    sine_part = jnp.sin(angles) * factor * sign_value
    top_pair = jnp.stack([cosine, sine_part])
    lower_edge_pair = jnp.stack([-sine_part, cosine])
    return jnp.stack([top_pair, lower_edge_pair])


def kernel_table(length):
    places = jnp.arange(length, dtype=jnp.int32)
    shifted = ((places + length // 2) % length - length // 2).astype(jnp.float32) / jnp.float32(
        length
    )
    squares = shifted[:, None] * shifted[:, None] + shifted[None, :] * shifted[None, :]
    phases = jnp.float32(-PHASE_SCALE * math.pi) * squares
    return jnp.stack([jnp.cos(phases), jnp.sin(phases)])


def complex_mul(leading_factor, factor_two):
    real_part = leading_factor[0] * factor_two[0] - leading_factor[1] * factor_two[1]
    imag_part = leading_factor[0] * factor_two[1] + leading_factor[1] * factor_two[0]
    return jnp.stack([real_part, imag_part])


def conj_mul(leading_factor, factor_two):
    real_part = leading_factor[0] * factor_two[0] + leading_factor[1] * factor_two[1]
    imag_part = leading_factor[0] * factor_two[1] - leading_factor[1] * factor_two[0]
    return jnp.stack([real_part, imag_part])


def transform(values, dft_matrix):
    initial_sweep = jnp.einsum("cjk,cdkl->djl", values, dft_matrix, precision=lax.Precision.HIGHEST)
    return jnp.einsum("xogs,xsn->ogn", dft_matrix, initial_sweep, precision=lax.Precision.HIGHEST)


def propagate(values, forward, inverse, kernel):
    spectrum = transform(values, forward)
    return transform(complex_mul(kernel, spectrum), inverse).astype(jnp.bfloat16)


def back_propagate(values, forward, inverse, kernel):
    spectrum = transform(values, forward)
    return transform(conj_mul(kernel, spectrum), inverse).astype(jnp.bfloat16)


def per_device(object_slices, probe, offsets, intensity):
    slice_count = object_slices.shape[0]
    tile_rows = object_slices.shape[2]
    length = probe.shape[-1]
    windows = offsets.shape[0]
    forward = dft_table(length, -1)
    inverse = dft_table(length, 1)
    kernel = kernel_table(length)
    zero_index = jnp.zeros((), jnp.int32)
    extended = padded(object_slices.astype(jnp.bfloat16), (("scan", 2),), HALO).astype(
        object_slices.dtype
    )

    def cut_patch(offset_pair):
        return lax.dynamic_slice(
            extended,
            (zero_index, zero_index, offset_pair[0], offset_pair[1]),
            (slice_count, 2, length, length),
        )

    patches = jax.vmap(cut_patch)(offsets)
    section_index = lax.axis_index("depth")
    depth_count = lax.axis_size("depth")
    last_section = depth_count - 1
    probe_wave = probe.astype(jnp.bfloat16)
    blank_wave = jnp.zeros((2, length, length), jnp.bfloat16)
    stored = jnp.zeros((windows, slice_count, 2, length, length), jnp.bfloat16)
    starts = jnp.zeros((windows, 2, length, length), jnp.bfloat16)
    turns_total = windows + depth_count - 1

    def forward_turn(step_tally, loop_state):
        received, stored_now, starts_now = loop_state
        window = step_tally - section_index
        active = (window >= 0) & (window < windows)
        slot_index = jnp.clip(window, 0, windows - 1)
        incoming = jnp.where(section_index == 0, probe_wave, received)

        def advance(nested_state):
            stored_in, starts_in = nested_state
            patch_set = lax.dynamic_index_in_dim(patches, slot_index, 0, keepdims=False)
            current = incoming
            stored_in = stored_in.at[slot_index, 0].set(current)
            product = complex_mul(current.astype(jnp.float32), patch_set[0])

            def far_field(values):
                far_wave = transform(values, forward)
                measured = lax.dynamic_index_in_dim(intensity, slot_index, 0, keepdims=False)
                residual = (
                    far_wave[0] * far_wave[0] + far_wave[1] * far_wave[1] - measured
                ) * far_wave
                return (blank_wave, transform(residual, inverse).astype(jnp.bfloat16))

            def onward(values):
                return (propagate(values, forward, inverse, kernel), blank_wave)

            current, start_grad = lax.cond(
                section_index == last_section, far_field, onward, product
            )
            starts_in = starts_in.at[slot_index].set(start_grad)
            return (current, stored_in, starts_in)

        def forward_pause(nested_state):
            return (blank_wave, nested_state[0], nested_state[1])

        outgoing, stored_now, starts_now = lax.cond(
            active, advance, forward_pause, (stored_now, starts_now)
        )
        received = from_behind(outgoing, "depth", 1)
        return (received, stored_now, starts_now)

    unused_wave, stored, starts = lax.fori_loop(
        0, turns_total, forward_turn, (blank_wave, stored, starts)
    )
    grad_area = jnp.zeros(extended.shape, jnp.float32)
    probe_sum = jnp.zeros((2, length, length), jnp.float32)

    def backward_turn(step_tally, loop_state):
        received, area_now, probe_now = loop_state
        window = step_tally - (last_section - section_index)
        active = (window >= 0) & (window < windows)
        slot_index = jnp.clip(window, 0, windows - 1)
        own_start = lax.dynamic_index_in_dim(starts, slot_index, 0, keepdims=False)
        incoming = jnp.where(section_index == last_section, own_start, received)

        def retreat(nested_state):
            grad_region, probe_in = nested_state
            patch_set = lax.dynamic_index_in_dim(patches, slot_index, 0, keepdims=False)
            wave_set = lax.dynamic_index_in_dim(stored, slot_index, 0, keepdims=False)
            current = incoming
            slice_grads = [None] * slice_count
            for level_index in reversed(range(slice_count)):
                grad_float = current.astype(jnp.float32)
                slice_grads[level_index] = conj_mul(
                    wave_set[level_index].astype(jnp.float32), grad_float
                )
                through = conj_mul(patch_set[level_index], grad_float)

                def to_probe(values):
                    return (blank_wave, probe_in + values)

                def upward(values):
                    return (back_propagate(values, forward, inverse, kernel), probe_in)

                current, probe_in = lax.cond(section_index == 0, to_probe, upward, through)
            stacked = jnp.stack(slice_grads)
            offset_pair = lax.dynamic_index_in_dim(offsets, slot_index, 0, keepdims=False)
            corner = (zero_index, zero_index, offset_pair[0], offset_pair[1])
            region = lax.dynamic_slice(grad_region, corner, (slice_count, 2, length, length))
            grad_region = lax.dynamic_update_slice(grad_region, region + stacked, corner)
            return (current, grad_region, probe_in)

        def backward_pause(nested_state):
            return (blank_wave, nested_state[0], nested_state[1])

        outgoing, area_now, probe_now = lax.cond(
            active, retreat, backward_pause, (area_now, probe_now)
        )
        received = from_behind(outgoing, "depth", -1)
        return (received, area_now, probe_now)

    unused_grad, grad_area, probe_sum = lax.fori_loop(
        0, turns_total, backward_turn, (blank_wave, grad_area, probe_sum)
    )
    own_rows = grad_area[:, :, HALO : HALO + tile_rows]
    upper_rim = grad_area[:, :, :HALO]
    lower_rim = grad_area[:, :, HALO + tile_rows :]
    from_next = passed_along(upper_rim.astype(jnp.bfloat16), "scan", -1).astype(upper_rim.dtype)
    from_prev = passed_along(lower_rim.astype(jnp.bfloat16), "scan", 1).astype(lower_rim.dtype)
    object_grad = own_rows + from_prev
    object_grad = object_grad + from_next
    partial_sum = lax.psum_scatter(
        probe_sum.astype(jnp.bfloat16), "depth", scatter_dimension=2, tiled=True
    )
    probe_grad = lax.psum_scatter(partial_sum, "scan", scatter_dimension=1, tiled=True).astype(
        jnp.float32
    )
    return (object_grad, probe_grad)


def solution(mesh):
    placed = (P("depth", None, "scan", None), P(), P("scan", None), P("scan", None, None))
    return jax.shard_map(
        per_device,
        mesh=mesh,
        in_specs=placed,
        out_specs=(P("depth", None, "scan", None), P(None, "scan", "depth")),
        check_vma=False,
    )
```

profile of v0, /device:TPU:2, one launch (start us, length us, event | category | flops | bytes accessed | tf_op | source)
XLA Modules:
  0.0 1335.8 jit_solution(10683571810433484882)
XLA Ops:
  10.2 5.8 collective-permute-start.3
  23.3 6.0 while.45
  31.0 347.1 %while.46 = (s32[]{:T(128)}, bf16[2,256,256]{2,1,0:T(8,128)(2,1)S(1)}, bf16[2,1,2,256,256]{4,3,2,1,0:T(8,128)(2,1)}, bf16[2,2,256,256]{2,3,1,0:T(8,128)(2,1)}, s...) while((s32[]{:T(128)}, ...), condition=%wide.region_7.8_spmd.clone.clone.clone, body=%wide.region_0.7_spmd.clone.clone.clone.sunk | while | flops 3223191552 | bytes 23073152 | solution.py:161
  31.3 20.9 %conditional.14 = (bf16[2,256,256]{2,1,0:T(8,128)(2,1)}, bf16[2,1,2,256,256]{4,3,2,1,0:T(8,128)(2,1)}, bf16[2,2,256,256]{2,3,1,0:T(8,128)(2,1)}) conditional(s32[]{:T(128)} %convert_element_type.211, (bf16[2,1,2,256,256]{4,3,2,1,0:T(8,128)(2,1)}, bf16[2,2,256,256]{2,3,1,0:T(8,128)(2,1)}) %tuple.193, (s32[]{:T(128)}, pred[]{:T(512)}, ...), branch_computations={%region_1.1_spmd, %region_2.6_spmd.clone} | conditional | flops 3223060480 | bytes 21761068 | solution.py:155
  35.3 10.5 conditional.10
  53.5 4.2 collective-permute-done
  57.8 20.9 %conditional.14 = (bf16[2,256,256]{2,1,0:T(8,128)(2,1)}, bf16[2,1,2,256,256]{4,3,2,1,0:T(8,128)(2,1)}, bf16[2,2,256,256]{2,3,1,0:T(8,128)(2,1)}) conditional(s32[]{:T(128)} %convert_element_type.211, (bf16[2,1,2,256,256]{4,3,2,1,0:T(8,128)(2,1)}, bf16[2,2,256,256]{2,3,1,0:T(8,128)(2,1)}) %tuple.193, (s32[]{:T(128)}, pred[]{:T(512)}, ...), branch_computations={%region_1.1_spmd, %region_2.6_spmd.clone} | conditional | flops 3223060480 | bytes 21761068 | solution.py:155
  61.8 10.5 conditional.10
  82.0 4.2 collective-permute-done
  87.0 23.4 %collective-permute-start = (bf16[2,256,256]{2,1,0:T(8,128)(2,1)}, bf16[2,256,256]{2,1,0:T(8,128)(2,1)S(1)}, u32[]{:S(2)}, u32[]{:S(2)}) collective-permute-start(bf16[2,256,256]{2,1,0:T(8,128)(2,1)} %get-tuple-element.1486), channel_id=1, source_target_pairs={{0,32},{32,64},{64,96},{96,128},{128,160},{160,192},{192,224},{224... | collective-permute-start | bytes 786440 | tf_op jit(solution)/shard_map/while/body/eval_jaxpr/ppermute | solution.py:33
  110.4 4.2 collective-permute-done
  115.4 4.3 collective-permute-start
  119.7 4.2 collective-permute-done
  124.8 21.6 %collective-permute-start = (bf16[2,256,256]{2,1,0:T(8,128)(2,1)}, bf16[2,256,256]{2,1,0:T(8,128)(2,1)S(1)}, u32[]{:S(2)}, u32[]{:S(2)}) collective-permute-start(bf16[2,256,256]{2,1,0:T(8,128)(2,1)} %get-tuple-element.1486), channel_id=1, source_target_pairs={{0,32},{32,64},{64,96},{96,128},{128,160},{160,192},{192,224},{224... | collective-permute-start | bytes 786440 | tf_op jit(solution)/shard_map/while/body/eval_jaxpr/ppermute | solution.py:33
  146.4 5.5 collective-permute-done
  152.8 4.3 collective-permute-start
  157.1 4.2 collective-permute-done
  162.1 23.0 %collective-permute-start = (bf16[2,256,256]{2,1,0:T(8,128)(2,1)}, bf16[2,256,256]{2,1,0:T(8,128)(2,1)S(1)}, u32[]{:S(2)}, u32[]{:S(2)}) collective-permute-start(bf16[2,256,256]{2,1,0:T(8,128)(2,1)} %get-tuple-element.1486), channel_id=1, source_target_pairs={{0,32},{32,64},{64,96},{96,128},{128,160},{160,192},{192,224},{224... | collective-permute-start | bytes 786440 | tf_op jit(solution)/shard_map/while/body/eval_jaxpr/ppermute | solution.py:33
  185.1 6.5 collective-permute-done
  192.5 4.3 collective-permute-start
  196.8 4.2 collective-permute-done
  201.8 23.1 %collective-permute-start = (bf16[2,256,256]{2,1,0:T(8,128)(2,1)}, bf16[2,256,256]{2,1,0:T(8,128)(2,1)S(1)}, u32[]{:S(2)}, u32[]{:S(2)}) collective-permute-start(bf16[2,256,256]{2,1,0:T(8,128)(2,1)} %get-tuple-element.1486), channel_id=1, source_target_pairs={{0,32},{32,64},{64,96},{96,128},{128,160},{160,192},{192,224},{224... | collective-permute-start | bytes 786440 | tf_op jit(solution)/shard_map/while/body/eval_jaxpr/ppermute | solution.py:33
  224.9 6.1 collective-permute-done
  231.9 4.3 collective-permute-start
  236.1 4.2 collective-permute-done
  241.2 17.9 %collective-permute-start = (bf16[2,256,256]{2,1,0:T(8,128)(2,1)}, bf16[2,256,256]{2,1,0:T(8,128)(2,1)S(1)}, u32[]{:S(2)}, u32[]{:S(2)}) collective-permute-start(bf16[2,256,256]{2,1,0:T(8,128)(2,1)} %get-tuple-element.1486), channel_id=1, source_target_pairs={{0,32},{32,64},{64,96},{96,128},{128,160},{160,192},{192,224},{224... | collective-permute-start | bytes 786440 | tf_op jit(solution)/shard_map/while/body/eval_jaxpr/ppermute | solution.py:33
  259.1 4.2 collective-permute-done
  264.1 4.8 collective-permute-start
  268.9 4.2 collective-permute-done
  273.9 17.9 %collective-permute-start = (bf16[2,256,256]{2,1,0:T(8,128)(2,1)}, bf16[2,256,256]{2,1,0:T(8,128)(2,1)S(1)}, u32[]{:S(2)}, u32[]{:S(2)}) collective-permute-start(bf16[2,256,256]{2,1,0:T(8,128)(2,1)} %get-tuple-element.1486), channel_id=1, source_target_pairs={{0,32},{32,64},{64,96},{96,128},{128,160},{160,192},{192,224},{224... | collective-permute-start | bytes 786440 | tf_op jit(solution)/shard_map/while/body/eval_jaxpr/ppermute | solution.py:33
  291.9 4.2 collective-permute-done
  296.9 5.5 collective-permute-start
  302.4 4.2 collective-permute-done
  307.5 19.4 %collective-permute-start = (bf16[2,256,256]{2,1,0:T(8,128)(2,1)}, bf16[2,256,256]{2,1,0:T(8,128)(2,1)S(1)}, u32[]{:S(2)}, u32[]{:S(2)}) collective-permute-start(bf16[2,256,256]{2,1,0:T(8,128)(2,1)} %get-tuple-element.1486), channel_id=1, source_target_pairs={{0,32},{32,64},{64,96},{96,128},{128,160},{160,192},{192,224},{224... | collective-permute-start | bytes 786440 | tf_op jit(solution)/shard_map/while/body/eval_jaxpr/ppermute | solution.py:33
  326.9 4.2 collective-permute-done
  331.9 5.5 collective-permute-start
  337.4 4.2 collective-permute-done
  342.4 31.5 %collective-permute-start = (bf16[2,256,256]{2,1,0:T(8,128)(2,1)}, bf16[2,256,256]{2,1,0:T(8,128)(2,1)S(1)}, u32[]{:S(2)}, u32[]{:S(2)}) collective-permute-start(bf16[2,256,256]{2,1,0:T(8,128)(2,1)} %get-tuple-element.1486), channel_id=1, source_target_pairs={{0,32},{32,64},{64,96},{96,128},{128,160},{160,192},{192,224},{224... | collective-permute-start | bytes 786440 | tf_op jit(solution)/shard_map/while/body/eval_jaxpr/ppermute | solution.py:33
  373.9 4.2 collective-permute-done
  382.1 673.9 %while.47 = (s32[]{:T(128)}, bf16[2,256,256]{1,2,0:T(8,128)(2,1)S(1)}, f32[1,2,384,384]{3,2,1,0:T(8,128)}, f32[2,256,256]{2,1,0:T(8,128)}, s32[]{:T(128)}, /*ind...) while((s32[]{:T(128)}, ...), condition=%wide.region_13.14_spmd.clone.clone.clone, body=%wide.region_8.13_spmd.clone.clone.clone.sunk | while | flops 3223584768 | bytes 23332560 | solution.py:211
  384.2 14.8 %collective-permute-done.1 = bf16[2,256,256]{1,2,0:T(8,128)(2,1)S(1)} collective-permute-done((bf16[2,256,256]{1,2,0:T(8,128)(2,1)}, bf16[2,256,256]{1,2,0:T(8,128)(2,1)S(1)}, u32[]{:S(2)}, u32[]{:S(2)}) %collective-permute-start.1) | collective-permute-done | bytes 262176 | tf_op jit(solution)/shard_map/while/body/eval_jaxpr/ppermute | solution.py:33
  401.2 12.1 collective-permute-done.1
  415.5 13.7 %collective-permute-done.1 = bf16[2,256,256]{1,2,0:T(8,128)(2,1)S(1)} collective-permute-done((bf16[2,256,256]{1,2,0:T(8,128)(2,1)}, bf16[2,256,256]{1,2,0:T(8,128)(2,1)S(1)}, u32[]{:S(2)}, u32[]{:S(2)}) %collective-permute-start.1) | collective-permute-done | bytes 262176 | tf_op jit(solution)/shard_map/while/body/eval_jaxpr/ppermute | solution.py:33
  431.3 15.7 %collective-permute-done.1 = bf16[2,256,256]{1,2,0:T(8,128)(2,1)S(1)} collective-permute-done((bf16[2,256,256]{1,2,0:T(8,128)(2,1)}, bf16[2,256,256]{1,2,0:T(8,128)(2,1)S(1)}, u32[]{:S(2)}, u32[]{:S(2)}) %collective-permute-start.1) | collective-permute-done | bytes 262176 | tf_op jit(solution)/shard_map/while/body/eval_jaxpr/ppermute | solution.py:33
  449.1 14.8 %collective-permute-done.1 = bf16[2,256,256]{1,2,0:T(8,128)(2,1)S(1)} collective-permute-done((bf16[2,256,256]{1,2,0:T(8,128)(2,1)}, bf16[2,256,256]{1,2,0:T(8,128)(2,1)S(1)}, u32[]{:S(2)}, u32[]{:S(2)}) %collective-permute-start.1) | collective-permute-done | bytes 262176 | tf_op jit(solution)/shard_map/while/body/eval_jaxpr/ppermute | solution.py:33
  466.1 17.0 %collective-permute-done.1 = bf16[2,256,256]{1,2,0:T(8,128)(2,1)S(1)} collective-permute-done((bf16[2,256,256]{1,2,0:T(8,128)(2,1)}, bf16[2,256,256]{1,2,0:T(8,128)(2,1)S(1)}, u32[]{:S(2)}, u32[]{:S(2)}) %collective-permute-start.1) | collective-permute-done | bytes 262176 | tf_op jit(solution)/shard_map/while/body/eval_jaxpr/ppermute | solution.py:33
  485.2 16.4 %collective-permute-done.1 = bf16[2,256,256]{1,2,0:T(8,128)(2,1)S(1)} collective-permute-done((bf16[2,256,256]{1,2,0:T(8,128)(2,1)}, bf16[2,256,256]{1,2,0:T(8,128)(2,1)S(1)}, u32[]{:S(2)}, u32[]{:S(2)}) %collective-permute-start.1) | collective-permute-done | bytes 262176 | tf_op jit(solution)/shard_map/while/body/eval_jaxpr/ppermute | solution.py:33
  503.7 16.6 %collective-permute-done.1 = bf16[2,256,256]{1,2,0:T(8,128)(2,1)S(1)} collective-permute-done((bf16[2,256,256]{1,2,0:T(8,128)(2,1)}, bf16[2,256,256]{1,2,0:T(8,128)(2,1)S(1)}, u32[]{:S(2)}, u32[]{:S(2)}) %collective-permute-start.1) | collective-permute-done | bytes 262176 | tf_op jit(solution)/shard_map/while/body/eval_jaxpr/ppermute | solution.py:33
  522.5 21.0 %collective-permute-done.1 = bf16[2,256,256]{1,2,0:T(8,128)(2,1)S(1)} collective-permute-done((bf16[2,256,256]{1,2,0:T(8,128)(2,1)}, bf16[2,256,256]{1,2,0:T(8,128)(2,1)S(1)}, u32[]{:S(2)}, u32[]{:S(2)}) %collective-permute-start.1) | collective-permute-done | bytes 262176 | tf_op jit(solution)/shard_map/while/body/eval_jaxpr/ppermute | solution.py:33
  545.7 10.7 collective-permute-done.1
  558.6 21.8 %collective-permute-done.1 = bf16[2,256,256]{1,2,0:T(8,128)(2,1)S(1)} collective-permute-done((bf16[2,256,256]{1,2,0:T(8,128)(2,1)}, bf16[2,256,256]{1,2,0:T(8,128)(2,1)S(1)}, u32[]{:S(2)}, u32[]{:S(2)}) %collective-permute-start.1) | collective-permute-done | bytes 262176 | tf_op jit(solution)/shard_map/while/body/eval_jaxpr/ppermute | solution.py:33
  582.5 10.0 collective-permute-done.1
  594.7 18.8 %collective-permute-done.1 = bf16[2,256,256]{1,2,0:T(8,128)(2,1)S(1)} collective-permute-done((bf16[2,256,256]{1,2,0:T(8,128)(2,1)}, bf16[2,256,256]{1,2,0:T(8,128)(2,1)S(1)}, u32[]{:S(2)}, u32[]{:S(2)}) %collective-permute-start.1) | collective-permute-done | bytes 262176 | tf_op jit(solution)/shard_map/while/body/eval_jaxpr/ppermute | solution.py:33
  615.6 9.2 collective-permute-done.1
  626.9 366.6 %collective-permute-done.1 = bf16[2,256,256]{1,2,0:T(8,128)(2,1)S(1)} collective-permute-done((bf16[2,256,256]{1,2,0:T(8,128)(2,1)}, bf16[2,256,256]{1,2,0:T(8,128)(2,1)S(1)}, u32[]{:S(2)}, u32[]{:S(2)}) %collective-permute-start.1) | collective-permute-done | bytes 262176 | tf_op jit(solution)/shard_map/while/body/eval_jaxpr/ppermute | solution.py:33
  993.7 20.5 %conditional.15 = (bf16[2,256,256]{1,2,0:T(8,128)(2,1)}, f32[1,2,384,384]{3,2,1,0:T(8,128)}, f32[2,256,256]{2,1,0:T(8,128)}) conditional(s32[]{:T(128)} %convert_element_type.212, (f32[1,2,384,384]{3,2,1,0:T(8,128)}, f32[2,256,256]{2,1,0:T(8,128)}) %tuple.196, (s32[]{:T(128)}, s32[]{:T(128)}, f32[2,1,2,256,256]{4,3,2,1,0:T(8,128)}, ...), branch_computations={%region_9.9_spmd, %region_10.12_spmd.clone} | conditional | flops 3223453696 | bytes 22020452 | solution.py:205
  1003.4 6.3 dynamic_update_slice.5
  1015.4 11.8 collective-permute-done.1
  1027.3 20.2 %conditional.15 = (bf16[2,256,256]{1,2,0:T(8,128)(2,1)}, f32[1,2,384,384]{3,2,1,0:T(8,128)}, f32[2,256,256]{2,1,0:T(8,128)}) conditional(s32[]{:T(128)} %convert_element_type.212, (f32[1,2,384,384]{3,2,1,0:T(8,128)}, f32[2,256,256]{2,1,0:T(8,128)}) %tuple.196, (s32[]{:T(128)}, s32[]{:T(128)}, f32[2,1,2,256,256]{4,3,2,1,0:T(8,128)}, ...), branch_computations={%region_9.9_spmd, %region_10.12_spmd.clone} | conditional | flops 3223453696 | bytes 22020452 | solution.py:205
  1037.1 6.1 dynamic_update_slice.5
  1048.8 7.2 collective-permute-done.1
  1059.3 5.8 collective-permute-start.5
  1072.7 150.2 %all-reduce.4.cloned.1.call-done = bf16[2,256,256]{1,0,2:T(2,128)(2,1)} async-done(((bf16[2,256,256]{1,0,2:T(2,128)(2,1)}), bf16[2,256,256]{1,0,2:T(2,128)(2,1)}) %all-reduce.4.cloned.1.call-update) | async-done | bytes 262160
  1223.8 104.5 %all-reduce.1 = bf16[2,256,16]{2,1,0:T(8,128)(2,1)S(1)} all-reduce(bf16[2,256,16]{2,1,0:T(8,128)(2,1)S(1)} %copy.31), channel_id=3, replica_groups=mesh['depth'=16,'scan'=32] {'scan'}, use_global_device_ids=true, to_apply=%region_15.16.clone | all-reduce | flops 8192 | bytes 32768
  (258 shorter events, 174.3 us)
Async XLA Ops:
  7.2 1215.8 %all-reduce.4.cloned.1.call-start = ((), (), s32[]{:S(2)}) async-start(), calls=%async_computation | async-start | bytes 524288
  8.2 13.9 %collective-permute-start.2 = (bf16[1,2,128,384]{3,2,1,0:T(8,128)(2,1)S(1)}, bf16[1,2,128,384]{3,2,1,0:T(8,128)(2,1)}, u32[]{:S(2)}, u32[]{:S(2)}) collective-permute-start(bf16[1,2,128,384]{3,2,1,0:T(8,128)(2,1)S(1)} %convert_element_type.153), channel_id=1, source_target_pairs={{0,1},{1,2},{2,3},{3,4},{4,5},{5,6},{6,7},{7,8},{8,9},{9,10},{10,1... | collective-permute-start | bytes 589832 | tf_op jit(solution)/shard_map/ppermute | solution.py:21
  10.2 12.0 collective-permute-start.3
  19.2 0.7 copy-start.8
  19.2 1.0 copy-start.6
  19.2 2.0 copy-start.5
  31.3 2.2 copy-start
  35.3 10.6 copy-start.7
  35.3 13.8 %copy-start.9 = (s32[5]{0:T(128)S(1)}, s32[5]{0:T(128)}, u32[]{:S(2)}) copy-start(s32[5]{0:T(128)} %constant.196.clone.1) | copy-start | bytes 64 | tf_op jit(solution)/shard_map/while/body/eval_jaxpr/cond
  35.3 14.5 %copy-start.1 = (bf16[2,256,256]{2,1,0:T(8,128)(2,1)S(1)}, bf16[2,256,256]{2,1,0:T(8,128)(2,1)}, u32[]{:S(2)}) copy-start(bf16[2,256,256]{2,1,0:T(8,128)(2,1)} %copy-done) | copy-start | bytes 786436 | tf_op jit(solution)/shard_map/while/body/eval_jaxpr/cond
  52.2 5.5 collective-permute-start
  57.8 2.2 copy-start
  61.8 10.6 copy-start.7
  61.8 13.8 %copy-start.9 = (s32[5]{0:T(128)S(1)}, s32[5]{0:T(128)}, u32[]{:S(2)}) copy-start(s32[5]{0:T(128)} %constant.196.clone.1) | copy-start | bytes 64 | tf_op jit(solution)/shard_map/while/body/eval_jaxpr/cond
  61.8 14.5 %copy-start.1 = (bf16[2,256,256]{2,1,0:T(8,128)(2,1)S(1)}, bf16[2,256,256]{2,1,0:T(8,128)(2,1)}, u32[]{:S(2)}) copy-start(bf16[2,256,256]{2,1,0:T(8,128)(2,1)} %copy-done) | copy-start | bytes 786436 | tf_op jit(solution)/shard_map/while/body/eval_jaxpr/cond
  78.7 7.4 collective-permute-start
  87.0 27.6 %collective-permute-start = (bf16[2,256,256]{2,1,0:T(8,128)(2,1)}, bf16[2,256,256]{2,1,0:T(8,128)(2,1)S(1)}, u32[]{:S(2)}, u32[]{:S(2)}) collective-permute-start(bf16[2,256,256]{2,1,0:T(8,128)(2,1)} %get-tuple-element.1486), channel_id=1, source_target_pairs={{0,32},{32,64},{64,96},{96,128},{128,160},{160,192},{192,224},{224... | collective-permute-start | bytes 786440 | tf_op jit(solution)/shard_map/while/body/eval_jaxpr/ppermute | solution.py:33
  115.4 8.5 collective-permute-start
  124.8 27.1 %collective-permute-start = (bf16[2,256,256]{2,1,0:T(8,128)(2,1)}, bf16[2,256,256]{2,1,0:T(8,128)(2,1)S(1)}, u32[]{:S(2)}, u32[]{:S(2)}) collective-permute-start(bf16[2,256,256]{2,1,0:T(8,128)(2,1)} %get-tuple-element.1486), channel_id=1, source_target_pairs={{0,32},{32,64},{64,96},{96,128},{128,160},{160,192},{192,224},{224... | collective-permute-start | bytes 786440 | tf_op jit(solution)/shard_map/while/body/eval_jaxpr/ppermute | solution.py:33
  152.8 8.5 collective-permute-start
  162.1 29.5 %collective-permute-start = (bf16[2,256,256]{2,1,0:T(8,128)(2,1)}, bf16[2,256,256]{2,1,0:T(8,128)(2,1)S(1)}, u32[]{:S(2)}, u32[]{:S(2)}) collective-permute-start(bf16[2,256,256]{2,1,0:T(8,128)(2,1)} %get-tuple-element.1486), channel_id=1, source_target_pairs={{0,32},{32,64},{64,96},{96,128},{128,160},{160,192},{192,224},{224... | collective-permute-start | bytes 786440 | tf_op jit(solution)/shard_map/while/body/eval_jaxpr/ppermute | solution.py:33
  192.5 8.5 collective-permute-start
  201.8 29.2 %collective-permute-start = (bf16[2,256,256]{2,1,0:T(8,128)(2,1)}, bf16[2,256,256]{2,1,0:T(8,128)(2,1)S(1)}, u32[]{:S(2)}, u32[]{:S(2)}) collective-permute-start(bf16[2,256,256]{2,1,0:T(8,128)(2,1)} %get-tuple-element.1486), channel_id=1, source_target_pairs={{0,32},{32,64},{64,96},{96,128},{128,160},{160,192},{192,224},{224... | collective-permute-start | bytes 786440 | tf_op jit(solution)/shard_map/while/body/eval_jaxpr/ppermute | solution.py:33
  231.9 8.5 collective-permute-start
  241.2 22.1 %collective-permute-start = (bf16[2,256,256]{2,1,0:T(8,128)(2,1)}, bf16[2,256,256]{2,1,0:T(8,128)(2,1)S(1)}, u32[]{:S(2)}, u32[]{:S(2)}) collective-permute-start(bf16[2,256,256]{2,1,0:T(8,128)(2,1)} %get-tuple-element.1486), channel_id=1, source_target_pairs={{0,32},{32,64},{64,96},{96,128},{128,160},{160,192},{192,224},{224... | collective-permute-start | bytes 786440 | tf_op jit(solution)/shard_map/while/body/eval_jaxpr/ppermute | solution.py:33
  264.1 9.0 collective-permute-start
  273.9 22.1 %collective-permute-start = (bf16[2,256,256]{2,1,0:T(8,128)(2,1)}, bf16[2,256,256]{2,1,0:T(8,128)(2,1)S(1)}, u32[]{:S(2)}, u32[]{:S(2)}) collective-permute-start(bf16[2,256,256]{2,1,0:T(8,128)(2,1)} %get-tuple-element.1486), channel_id=1, source_target_pairs={{0,32},{32,64},{64,96},{96,128},{128,160},{160,192},{192,224},{224... | collective-permute-start | bytes 786440 | tf_op jit(solution)/shard_map/while/body/eval_jaxpr/ppermute | solution.py:33
  296.9 9.7 collective-permute-start
  307.5 23.6 %collective-permute-start = (bf16[2,256,256]{2,1,0:T(8,128)(2,1)}, bf16[2,256,256]{2,1,0:T(8,128)(2,1)S(1)}, u32[]{:S(2)}, u32[]{:S(2)}) collective-permute-start(bf16[2,256,256]{2,1,0:T(8,128)(2,1)} %get-tuple-element.1486), channel_id=1, source_target_pairs={{0,32},{32,64},{64,96},{96,128},{128,160},{160,192},{192,224},{224... | collective-permute-start | bytes 786440 | tf_op jit(solution)/shard_map/while/body/eval_jaxpr/ppermute | solution.py:33
  331.9 9.7 collective-permute-start
  342.4 35.6 %collective-permute-start = (bf16[2,256,256]{2,1,0:T(8,128)(2,1)}, bf16[2,256,256]{2,1,0:T(8,128)(2,1)S(1)}, u32[]{:S(2)}, u32[]{:S(2)}) collective-permute-start(bf16[2,256,256]{2,1,0:T(8,128)(2,1)} %get-tuple-element.1486), channel_id=1, source_target_pairs={{0,32},{32,64},{64,96},{96,128},{128,160},{160,192},{192,224},{224... | collective-permute-start | bytes 786440 | tf_op jit(solution)/shard_map/while/body/eval_jaxpr/ppermute | solution.py:33
  382.9 16.1 %collective-permute-start.1 = (bf16[2,256,256]{1,2,0:T(8,128)(2,1)}, bf16[2,256,256]{1,2,0:T(8,128)(2,1)S(1)}, u32[]{:S(2)}, u32[]{:S(2)}) collective-permute-start(bf16[2,256,256]{1,2,0:T(8,128)(2,1)} %get-tuple-element.1503), channel_id=1, source_target_pairs={{32,0},{64,32},{96,64},{128,96},{160,128},{192,160},{224,192},{256... | collective-permute-start | bytes 786440 | tf_op jit(solution)/shard_map/while/body/eval_jaxpr/ppermute | solution.py:33
  399.9 13.4 %collective-permute-start.1 = (bf16[2,256,256]{1,2,0:T(8,128)(2,1)}, bf16[2,256,256]{1,2,0:T(8,128)(2,1)S(1)}, u32[]{:S(2)}, u32[]{:S(2)}) collective-permute-start(bf16[2,256,256]{1,2,0:T(8,128)(2,1)} %get-tuple-element.1503), channel_id=1, source_target_pairs={{32,0},{64,32},{96,64},{128,96},{160,128},{192,160},{224,192},{256... | collective-permute-start | bytes 786440 | tf_op jit(solution)/shard_map/while/body/eval_jaxpr/ppermute | solution.py:33
  414.2 15.0 %collective-permute-start.1 = (bf16[2,256,256]{1,2,0:T(8,128)(2,1)}, bf16[2,256,256]{1,2,0:T(8,128)(2,1)S(1)}, u32[]{:S(2)}, u32[]{:S(2)}) collective-permute-start(bf16[2,256,256]{1,2,0:T(8,128)(2,1)} %get-tuple-element.1503), channel_id=1, source_target_pairs={{32,0},{64,32},{96,64},{128,96},{160,128},{192,160},{224,192},{256... | collective-permute-start | bytes 786440 | tf_op jit(solution)/shard_map/while/body/eval_jaxpr/ppermute | solution.py:33
  430.0 17.0 %collective-permute-start.1 = (bf16[2,256,256]{1,2,0:T(8,128)(2,1)}, bf16[2,256,256]{1,2,0:T(8,128)(2,1)S(1)}, u32[]{:S(2)}, u32[]{:S(2)}) collective-permute-start(bf16[2,256,256]{1,2,0:T(8,128)(2,1)} %get-tuple-element.1503), channel_id=1, source_target_pairs={{32,0},{64,32},{96,64},{128,96},{160,128},{192,160},{224,192},{256... | collective-permute-start | bytes 786440 | tf_op jit(solution)/shard_map/while/body/eval_jaxpr/ppermute | solution.py:33
  447.9 16.1 %collective-permute-start.1 = (bf16[2,256,256]{1,2,0:T(8,128)(2,1)}, bf16[2,256,256]{1,2,0:T(8,128)(2,1)S(1)}, u32[]{:S(2)}, u32[]{:S(2)}) collective-permute-start(bf16[2,256,256]{1,2,0:T(8,128)(2,1)} %get-tuple-element.1503), channel_id=1, source_target_pairs={{32,0},{64,32},{96,64},{128,96},{160,128},{192,160},{224,192},{256... | collective-permute-start | bytes 786440 | tf_op jit(solution)/shard_map/while/body/eval_jaxpr/ppermute | solution.py:33
  464.8 18.3 %collective-permute-start.1 = (bf16[2,256,256]{1,2,0:T(8,128)(2,1)}, bf16[2,256,256]{1,2,0:T(8,128)(2,1)S(1)}, u32[]{:S(2)}, u32[]{:S(2)}) collective-permute-start(bf16[2,256,256]{1,2,0:T(8,128)(2,1)} %get-tuple-element.1503), channel_id=1, source_target_pairs={{32,0},{64,32},{96,64},{128,96},{160,128},{192,160},{224,192},{256... | collective-permute-start | bytes 786440 | tf_op jit(solution)/shard_map/while/body/eval_jaxpr/ppermute | solution.py:33
  483.9 17.7 %collective-permute-start.1 = (bf16[2,256,256]{1,2,0:T(8,128)(2,1)}, bf16[2,256,256]{1,2,0:T(8,128)(2,1)S(1)}, u32[]{:S(2)}, u32[]{:S(2)}) collective-permute-start(bf16[2,256,256]{1,2,0:T(8,128)(2,1)} %get-tuple-element.1503), channel_id=1, source_target_pairs={{32,0},{64,32},{96,64},{128,96},{160,128},{192,160},{224,192},{256... | collective-permute-start | bytes 786440 | tf_op jit(solution)/shard_map/while/body/eval_jaxpr/ppermute | solution.py:33
  502.5 17.9 %collective-permute-start.1 = (bf16[2,256,256]{1,2,0:T(8,128)(2,1)}, bf16[2,256,256]{1,2,0:T(8,128)(2,1)S(1)}, u32[]{:S(2)}, u32[]{:S(2)}) collective-permute-start(bf16[2,256,256]{1,2,0:T(8,128)(2,1)} %get-tuple-element.1503), channel_id=1, source_target_pairs={{32,0},{64,32},{96,64},{128,96},{160,128},{192,160},{224,192},{256... | collective-permute-start | bytes 786440 | tf_op jit(solution)/shard_map/while/body/eval_jaxpr/ppermute | solution.py:33
  521.2 22.3 %collective-permute-start.1 = (bf16[2,256,256]{1,2,0:T(8,128)(2,1)}, bf16[2,256,256]{1,2,0:T(8,128)(2,1)S(1)}, u32[]{:S(2)}, u32[]{:S(2)}) collective-permute-start(bf16[2,256,256]{1,2,0:T(8,128)(2,1)} %get-tuple-element.1503), channel_id=1, source_target_pairs={{32,0},{64,32},{96,64},{128,96},{160,128},{192,160},{224,192},{256... | collective-permute-start | bytes 786440 | tf_op jit(solution)/shard_map/while/body/eval_jaxpr/ppermute | solution.py:33
  544.4 12.0 collective-permute-start.1
  557.3 23.0 %collective-permute-start.1 = (bf16[2,256,256]{1,2,0:T(8,128)(2,1)}, bf16[2,256,256]{1,2,0:T(8,128)(2,1)S(1)}, u32[]{:S(2)}, u32[]{:S(2)}) collective-permute-start(bf16[2,256,256]{1,2,0:T(8,128)(2,1)} %get-tuple-element.1503), channel_id=1, source_target_pairs={{32,0},{64,32},{96,64},{128,96},{160,128},{192,160},{224,192},{256... | collective-permute-start | bytes 786440 | tf_op jit(solution)/shard_map/while/body/eval_jaxpr/ppermute | solution.py:33
  581.2 11.3 collective-permute-start.1
  593.4 20.1 %collective-permute-start.1 = (bf16[2,256,256]{1,2,0:T(8,128)(2,1)}, bf16[2,256,256]{1,2,0:T(8,128)(2,1)S(1)}, u32[]{:S(2)}, u32[]{:S(2)}) collective-permute-start(bf16[2,256,256]{1,2,0:T(8,128)(2,1)} %get-tuple-element.1503), channel_id=1, source_target_pairs={{32,0},{64,32},{96,64},{128,96},{160,128},{192,160},{224,192},{256... | collective-permute-start | bytes 786440 | tf_op jit(solution)/shard_map/while/body/eval_jaxpr/ppermute | solution.py:33
  614.3 10.5 collective-permute-start.1
  625.6 367.9 %collective-permute-start.1 = (bf16[2,256,256]{1,2,0:T(8,128)(2,1)}, bf16[2,256,256]{1,2,0:T(8,128)(2,1)S(1)}, u32[]{:S(2)}, u32[]{:S(2)}) collective-permute-start(bf16[2,256,256]{1,2,0:T(8,128)(2,1)} %get-tuple-element.1503), channel_id=1, source_target_pairs={{32,0},{64,32},{96,64},{128,96},{160,128},{192,160},{224,192},{256... | collective-permute-start | bytes 786440 | tf_op jit(solution)/shard_map/while/body/eval_jaxpr/ppermute | solution.py:33
  1002.0 7.8 copy-start.2
  1002.0 7.8 copy-start.3
  1014.1 13.1 collective-permute-start.1
  1035.7 7.5 copy-start.2
  1035.7 7.5 copy-start.3
  1047.5 8.5 collective-permute-start.1
  1057.4 13.5 %collective-permute-start.4 = (bf16[1,2,128,384]{3,2,1,0:T(8,128)(2,1)S(1)}, bf16[1,2,128,384]{3,2,1,0:T(8,128)(2,1)S(1)}, u32[]{:S(2)}, u32[]{:S(2)}) collective-permute-start(bf16[1,2,128,384]{3,2,1,0:T(8,128)(2,1)S(1)} %get-tuple-element.1295), channel_id=1, source_target_pairs={{31,0},{0,1},{1,2},{2,3},{3,4},{4,5},{5,6},{6,7},{7,8},{8,9},{9,10... | collective-permute-start | bytes 589832 | tf_op jit(solution)/shard_map/ppermute | solution.py:39
  1059.3 11.6 collective-permute-start.5
Sparse Core Ops, SparseCore 0:
  1067.2 155.7 all-reduce.3
where the time goes:
time: 1340 us
  waiting for transfers between devices  825 us (62%)
  starting transfers between devices  252 us (19%)
  blocking collectives  105 us (8%)
  local copies, waits for them, and re-layouts  70.2 us (5%)
  other arithmetic  47.4 us (4%)
  between operations  15.5 us (1%)
    ppermute x34, waiting for transfers between devices, from_behind(): return lax.ppermute(block, axis, route)  675 us
    ppermute x34, starting transfers between devices, from_behind(): return lax.ppermute(block, axis, route)  237 us
    unnamed x2, waiting for transfers between devices  150 us
    unnamed x1, blocking collectives  105 us
  transfers between devices with their start and end apart: 39, of which 35 were waited for; matrix products, arithmetic and copies ran while one was open for 1% of the time, Pallas kernels for 0%

commit v1 on v0

v1 whole, which is shorter than its diff:
```python
import functools
import math

import jax
import jax.numpy as jnp
import ml_dtypes
import numpy as np
from jax import lax
from jax.experimental import pallas as pl
from jax.experimental.pallas import tpu as pltpu
from jax.sharding import PartitionSpec as P

MESH = pl.DeviceIdType.MESH
N = 256
HALF = 128
TILE = 128
COLS = 384
SLICES = 16
PHASE_SCALE = 16.0
BF = jnp.bfloat16
F32 = jnp.float32


def real_form(table):
    return np.block([[table.real, table.imag], [-table.imag, table.real]])


def tables():
    n = np.arange(N)
    dft = np.exp(-2j * math.pi * (np.outer(n, n) % N) / N) / math.sqrt(N)
    q = ((n + HALF) % N - HALF) / N
    circulant = dft.conj() @ np.diag(np.exp(-1j * PHASE_SCALE * math.pi * q * q)) @ dft
    upper, lower = circulant[:HALF, :HALF], circulant[HALF:, :HALF]
    right = [
        real_form((upper + lower) / 2),
        real_form((upper - lower) / 2),
        real_form(dft[:HALF, 0::2]),
        real_form(dft[:HALF, 1::2]),
    ]
    full = np.stack(right + [t.T for t in right]).astype(np.float32)
    high = full.astype(ml_dtypes.bfloat16)
    low = (full - high.astype(np.float32)).astype(ml_dtypes.bfloat16)
    return np.stack([high, low], axis=1)


def dot(a, b):
    return jnp.dot(a, b, preferred_element_type=F32)


def one_hot(shape, hit):
    r = lax.broadcasted_iota(jnp.int32, shape, 0)
    c = lax.broadcasted_iota(jnp.int32, shape, 1)
    return jnp.where(hit(r, c), 1.0, 0.0).astype(BF)


def halves(x, axis):
    if axis == 0:
        return x[:HALF], x[HALF:]
    return x[:, :HALF], x[:, HALF:]


def butterfly(x, axis):
    first, second = halves(x, axis)
    return first + second, first - second


def join(a, b, axis):
    return jnp.concatenate([a, b], axis=axis)


def right_mul(x, tab, k):
    x = x.astype(BF)
    return dot(x, tab[k, 0]) + dot(x, tab[k, 1])


def left_mul(x, tab, k):
    x = x.astype(BF)
    return dot(tab[k, 0], x) + dot(tab[k, 1], x)


def columns_in(re, im, tab, k):
    sr, dr = butterfly(re, 1)
    si, di = butterfly(im, 1)
    a = right_mul(join(sr, si, 1), tab, k)
    b = right_mul(join(dr, di, 1), tab, k + 1)
    ar, ai = halves(a, 1)
    br, bi = halves(b, 1)
    return join(ar, br, 1), join(ai, bi, 1)


def rows_in(re, im, tab, k):
    sr, dr = butterfly(re, 0)
    si, di = butterfly(im, 0)
    a = left_mul(join(sr, si, 0), tab, k)
    b = left_mul(join(dr, di, 0), tab, k + 1)
    ar, ai = halves(a, 0)
    br, bi = halves(b, 0)
    return join(ar, br, 0), join(ai, bi, 0)


def rows_out(re, im, tab, k):
    re0, re1 = halves(re, 0)
    im0, im1 = halves(im, 0)
    a = left_mul(join(re0, im0, 0), tab, k)
    b = left_mul(join(re1, im1, 0), tab, k + 1)
    ar, ai = halves(a, 0)
    br, bi = halves(b, 0)
    return join(ar + br, ar - br, 0), join(ai + bi, ai - bi, 0)


def columns_out(re, im, tab, k):
    re0, re1 = halves(re, 1)
    im0, im1 = halves(im, 1)
    a = right_mul(join(re0, im0, 1), tab, k)
    b = right_mul(join(re1, im1, 1), tab, k + 1)
    ar, ai = halves(a, 1)
    br, bi = halves(b, 1)
    return join(ar + br, ar - br, 1), join(ai + bi, ai - bi, 1)


def propagate(re, im, tab, right, left):
    re, im = columns_in(re, im, tab, right)
    re, im = rows_in(re, im, tab, left)
    re, im = join(*butterfly(re, 0), 0), join(*butterfly(im, 0), 0)
    return join(*butterfly(re, 1), 1), join(*butterfly(im, 1), 1)


def remote(src, dst, send, recv, axis, index):
    return pltpu.make_async_remote_copy(
        src_ref=src,
        dst_ref=dst,
        send_sem=send,
        recv_sem=recv,
        device_id={axis: index},
        device_id_type=MESH,
    )


def kernel(
    off_ref, obj_ref, probe_ref, int_ref, tab_hbm,
    out_ref, part_ref,
    region, patch, held, waves, current, gout, gin, rim, rim_in, tab, meas,
    halo_send, halo_recv, patch_send, patch_recv, grad_send, grad_recv, rim_send, rim_recv, local_sem,
):
    d = lax.axis_index("depth")
    m = lax.axis_index("scan")
    above, below = lax.rem(m + 31, 32), lax.rem(m + 1, 32)
    core = lax.rem(m, 2)
    x_lo = m // 16
    worker = [j * 8 + lax.rem(4 * core + 2 * j + x_lo, 8) for j in range(2)]
    mine = [d == w for w in worker]
    working = jnp.logical_or(mine[0], mine[1])

    tab_copy = pltpu.make_async_copy(tab_hbm, tab, local_sem.at[0])
    meas_copy = [pltpu.make_async_copy(int_ref.at[j], meas, local_sem.at[1]) for j in range(2)]

    @pl.when(working)
    def _():
        tab_copy.start()

    for j in range(2):

        @pl.when(mine[j])
        def _():
            meas_copy[j].start()

    barrier = pltpu.get_barrier_semaphore()
    for t in (above, below):
        pl.semaphore_signal(barrier, inc=1, device_id={"scan": t}, device_id_type=MESH)
    for j in range(2):

        @pl.when(jnp.logical_not(mine[j]))
        def _():
            pl.semaphore_signal(barrier, inc=1, device_id={"depth": worker[j]}, device_id_type=MESH)

    region[1] = obj_ref[0].astype(BF)

    @pl.when(working)
    def _():
        def greet(k, c):
            @pl.when(jnp.logical_and(k != worker[0], k != worker[1]))
            def _():
                pl.semaphore_signal(barrier, inc=1, device_id={"depth": k}, device_id_type=MESH)

            return c

        lax.fori_loop(0, SLICES, greet, 0)
        pl.semaphore_wait(barrier, 17)

    @pl.when(jnp.logical_not(working))
    def _():
        pl.semaphore_wait(barrier, 4)

    down = remote(region.at[1], region.at[0], halo_send.at[0], halo_recv.at[0], "scan", below)
    up = remote(region.at[1], region.at[2], halo_send.at[1], halo_recv.at[1], "scan", above)
    down.start()
    up.start()
    row_off = [off_ref[j, 0] for j in range(2)]
    col_off = [off_ref[j, 1] for j in range(2)]
    pick_cols = join(
        *[one_hot((COLS, N), lambda r, c, j=j: r == c + col_off[j]) for j in range(2)], 1
    )
    pick_rows = [one_hot((N, 3 * TILE), lambda r, c, j=j: c == r + row_off[j]) for j in range(2)]
    down.wait_recv()
    up.wait_recv()
    for c in range(2):
        strip = jnp.concatenate([region[t, c] for t in range(3)], axis=0)
        narrow = dot(strip, pick_cols).astype(BF)
        for j in range(2):
            patch[j, c] = dot(pick_rows[j], narrow[:, j * N : (j + 1) * N]).astype(BF)

    def patch_copy(j):
        return remote(patch.at[j], held.at[d], patch_send.at[j], patch_recv.at[d], "depth", worker[j])

    def patch_keep(j):
        return pltpu.make_async_copy(patch.at[j], held.at[d], patch_recv.at[d])

    for j in range(2):

        @pl.when(mine[j])
        def _():
            patch_keep(j).start()

        @pl.when(jnp.logical_not(mine[j]))
        def _():
            patch_copy(j).start()

    down.wait_send()
    up.wait_send()

    def work(j):
        tab_copy.wait()
        meas_copy[j].wait()
        even_odd = one_hot(
            (N, N),
            lambda r, c: c == jnp.where(r < HALF, 2 * r, 2 * r - (N - 1)),
        )
        even_odd_t = one_hot(
            (N, N),
            lambda r, c: r == jnp.where(c < HALF, 2 * c, 2 * c - (N - 1)),
        )
        measured = meas[...]
        high = measured.astype(BF)
        low = (measured - high.astype(F32)).astype(BF)
        meas[...] = dot(dot(even_odd, high).astype(BF), even_odd_t) + dot(
            dot(even_odd, low).astype(BF), even_odd_t
        )
        for c in range(2):
            current[c] = probe_ref[c].astype(BF).astype(F32)

        def wait_patch(s):
            @pl.when(s == d)
            def _():
                patch_keep(j).wait()

            @pl.when(s != d)
            def _():
                remote(
                    patch.at[j], held.at[s], patch_send.at[j], patch_recv.at[s], "depth", worker[j]
                ).wait_recv()

        def exit_wave(s):
            wait_patch(s)
            wr, wi = current[0], current[1]
            waves[s, 0] = wr.astype(BF)
            waves[s, 1] = wi.astype(BF)
            pr, pi = held[s, 0].astype(F32), held[s, 1].astype(F32)
            return wr * pr - wi * pi, wr * pi + wi * pr

        def forward(s, carry):
            re, im = exit_wave(s)
            re, im = propagate(re, im, tab, 0, 4)
            current[0] = re
            current[1] = im
            return carry

        lax.fori_loop(0, SLICES - 1, forward, 0)
        re, im = exit_wave(SLICES - 1)
        re, im = columns_in(re, im, tab, 2)
        re, im = rows_in(re, im, tab, 6)
        misfit = re * re + im * im - meas[...]
        re, im = rows_out(misfit * re, misfit * im, tab, 2)
        re, im = columns_out(re, im, tab, 6)
        current[0] = re
        current[1] = im

        def grad_copy(s):
            return remote(gout.at[s], gin.at[j], grad_send.at[s], grad_recv.at[j], "depth", s)

        def grad_keep(s):
            return pltpu.make_async_copy(gout.at[s], gin.at[j], grad_recv.at[j])

        def through(s):
            gr, gi = current[0], current[1]
            wr, wi = waves[s, 0].astype(F32), waves[s, 1].astype(F32)
            gout[s, 0] = (wr * gr + wi * gi).astype(BF)
            gout[s, 1] = (wr * gi - wi * gr).astype(BF)

            @pl.when(s == d)
            def _():
                grad_keep(s).start()

            @pl.when(s != d)
            def _():
                grad_copy(s).start()

            pr, pi = held[s, 0].astype(F32), held[s, 1].astype(F32)
            return pr * gr + pi * gi, pr * gi - pi * gr

        def backward(i, carry):
            re, im = through(SLICES - 1 - i)
            re, im = propagate(re, im, tab, 4, 0)
            current[0] = re
            current[1] = im
            return carry

        lax.fori_loop(0, SLICES - 1, backward, 0)
        re, im = through(0)
        part_ref[0] = re
        part_ref[1] = im

        def sent(s, carry):
            @pl.when(s != d)
            def _():
                grad_copy(s).wait_send()

            return carry

        lax.fori_loop(0, SLICES, sent, 0)

    for j in range(2):

        @pl.when(mine[j])
        def _():
            work(j)

    @pl.when(jnp.logical_not(working))
    def _():
        part_ref[...] = jnp.zeros_like(part_ref)

    for j in range(2):

        @pl.when(jnp.logical_not(mine[j]))
        def _():
            patch_copy(j).wait_send()
            remote(gout.at[0], gin.at[j], grad_send.at[0], grad_recv.at[j], "depth", d).wait_recv()

        @pl.when(mine[j])
        def _():
            pltpu.make_async_copy(gout.at[d], gin.at[j], grad_recv.at[j]).wait()

    put_cols = [one_hot((N, COLS), lambda r, c, j=j: c == r + col_off[j]) for j in range(2)]
    put_rows = join(
        *[one_hot((3 * TILE, N), lambda r, c, j=j: r == c + row_off[j]) for j in range(2)], 1
    )
    for c in range(2):
        wide = join(*[dot(gin[j, c], put_cols[j]).astype(BF) for j in range(2)], 0)
        total = dot(put_rows, wide)
        rim[0, c] = total[:TILE].astype(BF)
        rim[1, c] = total[2 * TILE :].astype(BF)
        out_ref[0, c] = total[TILE : 2 * TILE]
    to_above = remote(rim.at[0], rim_in.at[0], rim_send.at[0], rim_recv.at[0], "scan", above)
    to_below = remote(rim.at[1], rim_in.at[1], rim_send.at[1], rim_recv.at[1], "scan", below)
    to_above.start()
    to_below.start()
    to_above.wait_recv()
    to_below.wait_recv()
    out_ref[0] = out_ref[0] + rim_in[0].astype(F32) + rim_in[1].astype(F32)
    to_above.wait_send()
    to_below.wait_send()


def per_device(tab, object_slices, probe, offsets, intensity):
    vmem = pl.BlockSpec(memory_space=pltpu.VMEM)
    plane = (2, N, N)
    object_grad, part = pl.pallas_call(
        kernel,
        out_shape=(
            jax.ShapeDtypeStruct(object_slices.shape, F32),
            jax.ShapeDtypeStruct(plane, F32),
        ),
        in_specs=[
            pl.BlockSpec(memory_space=pltpu.SMEM),
            vmem,
            vmem,
            pl.BlockSpec(memory_space=pl.ANY),
            pl.BlockSpec(memory_space=pl.ANY),
        ],
        out_specs=(vmem, vmem),
        scratch_shapes=[
            pltpu.VMEM((3, 2, TILE, COLS), BF),
            pltpu.VMEM((2, *plane), BF),
            pltpu.VMEM((SLICES, *plane), BF),
            pltpu.VMEM((SLICES, *plane), BF),
            pltpu.VMEM(plane, F32),
            pltpu.VMEM((SLICES, *plane), BF),
            pltpu.VMEM((2, *plane), BF),
            pltpu.VMEM((2, 2, TILE, COLS), BF),
            pltpu.VMEM((2, 2, TILE, COLS), BF),
            pltpu.VMEM((8, 2, N, N), BF),
            pltpu.VMEM((N, N), F32),
            pltpu.SemaphoreType.DMA((2,)),
            pltpu.SemaphoreType.DMA((2,)),
            pltpu.SemaphoreType.DMA((2,)),
            pltpu.SemaphoreType.DMA((SLICES,)),
            pltpu.SemaphoreType.DMA((SLICES,)),
            pltpu.SemaphoreType.DMA((2,)),
            pltpu.SemaphoreType.DMA((2,)),
            pltpu.SemaphoreType.DMA((2,)),
            pltpu.SemaphoreType.DMA((2,)),
        ],
        compiler_params=pltpu.CompilerParams(
            collective_id=0, has_side_effects=True, vmem_limit_bytes=48 << 20
        ),
        name="ptychography_chains",
    )(offsets, object_slices, probe, intensity, tab)
    partial_sum = lax.psum_scatter(part.astype(BF), "depth", scatter_dimension=2, tiled=True)
    probe_grad = lax.psum_scatter(partial_sum, "scan", scatter_dimension=1, tiled=True)
    return object_grad, probe_grad.astype(F32)


def solution(mesh):
    tab = tables()
    placed = (P("depth", None, "scan", None), P(), P("scan", None), P("scan", None, None))
    return jax.shard_map(
        lambda *args: per_device(jnp.asarray(tab), *args),
        mesh=mesh,
        in_specs=placed,
        out_specs=(P("depth", None, "scan", None), P(None, "scan", "depth")),
        check_vma=False,
    )
```

time: 1340 us -> 371 us (0.28)
  waiting for transfers between devices: 825 us -> 152 us
  starting transfers between devices: 252 us -> 0.04 us
  Pallas kernels: 0 us -> 87.7 us
  local copies, waits for them, and re-layouts: 70.2 us -> 10.4 us
  other arithmetic: 47.4 us -> 0.63 us
    ppermute x38 -> x0, waiting for transfers between devices: 675 us -> none  [the longest x34 675 us: from_behind(): return lax.ppermute(block, axis, route)]
    ppermute x38 -> x0, starting transfers between devices: 252 us -> none  [the longest x34 237 us: from_behind(): return lax.ppermute(block, axis, route)]
    pallas_call x0 -> x1, Pallas kernels: none -> 87.7 us  [per_device(): pl.pallas_call(kernel, out_shape=(jax.ShapeDtypeStruct(object_slices.shap...]
    broadcast_in_dim x38 -> x0, local copies, waits for them, and re-layouts: 27 us -> none  [the longest x34 23.4 us: per_device(): blank_wave = jnp.zeros((2, length, length), jnp.bfloat16)]
  transfers between devices with their start and end apart: 39 -> 1, of which waited for: 35 -> 1; matrix products, arithmetic and copies ran while one was open for 1% -> 1% of each run, Pallas kernels for 0% -> 0%
where the time goes in v1:
time: 371 us; the launch traced here: 370 us
  waiting for transfers between devices  152 us (41%)
  blocking collectives  105 us (28%)
  Pallas kernels  87.7 us (24%)
  between operations  15.4 us (4%)
  local copies, waits for them, and re-layouts  10.4 us (3%)
    unnamed x2, waiting for transfers between devices  152 us
    unnamed x1, blocking collectives  105 us
    pallas_call x1, Pallas kernels, per_device(): pl.pallas_call(kernel, out_shape=(jax.ShapeDtypeStruct(object_slices.shap...  87.7 us
    unnamed x14, local copies, waits for them, and re-layouts  9.43 us
  transfers between devices with their start and end apart: 1, of which 1 were waited for; matrix products, arithmetic and copies ran while one was open for 1% of the time, Pallas kernels for 0%

profile of v1, /device:TPU:2, one launch (start us, length us, event | category | flops | bytes accessed | tf_op | source)
XLA Modules:
  0.0 370.4 jit_solution(9320431929232559215)
XLA Ops:
  7.2 0.0 all-reduce.4.cloned.1.call-start
  7.2 0.0 copy-start
  7.2 1.6 copy-done
  8.8 0.0 copy-start.1
  8.8 1.0 copy-done.1
  9.8 0.0 copy-start.2
  9.8 1.0 copy-done.2
  10.9 0.0 copy-start.3
  10.9 1.0 copy-done.3
  11.9 0.0 copy-start.4
  11.9 0.7 copy-done.4
  12.6 87.7 %ptychography_chains.1 = (f32[1,2,128,384]{3,2,1,0:T(8,128)S(1)}, f32[2,256,256]{2,1,0:T(8,128)S(1)}) custom-call(s32[2,2]{1,0:T(2,128)S(1)} %copy-done.4, f32[1,2,128,384]{3,2,1,0:T(8,128)S(1)} %copy-done.3, f32[2,256,256]{2,1,0:T(8,128)S(1)} %copy-done.1, f32[2,256,256]{2,1,0:T(8,128)S(1)} %copy-done.2, bf16[8,2,256,256]{3,2,1,0:T(8,128)(2,1)S(1)} %copy-done), custom_call_target="tpu_custom_call" | custom-call | tf_op jit(solution)/shard_map/ptychography_chains/pallas_call | solution.py:376
  100.3 0.9 copy.7
  101.2 0.0 all-reduce.4.cloned.1.call-update
  101.2 1.3 dynamic-slice
  102.5 1.3 dynamic-slice.2
  105.1 151.7 %all-reduce.4.cloned.1.call-done = bf16[2,256,256]{1,0,2:T(2,128)(2,1)} async-done(((bf16[2,256,256]{1,0,2:T(2,128)(2,1)}), bf16[2,256,256]{1,0,2:T(2,128)(2,1)}) %all-reduce.4.cloned.1.call-update) | async-done | bytes 262160
  256.9 0.7 constant_dynamic-slice_fusion
  257.6 0.1 copy.8
  257.7 104.5 %all-reduce.1 = bf16[2,256,16]{2,1,0:T(8,128)(2,1)S(1)} all-reduce(bf16[2,256,16]{2,1,0:T(8,128)(2,1)S(1)} %copy.8), channel_id=3, replica_groups=mesh['depth'=16,'scan'=32] {'scan'}, use_global_device_ids=true, to_apply=%region_1.0.clone | all-reduce | flops 8192 | bytes 32768
  362.2 0.6 dynamic-slice_convert_fusion
  362.8 0.7 copy.13
  (1 shorter events, 0.0 us)
Async XLA Ops:
  7.2 249.7 %all-reduce.4.cloned.1.call-start = ((), (), s32[]{:S(2)}) async-start(), calls=%async_computation | async-start | bytes 524288
  7.2 1.6 copy-start
  8.8 1.0 copy-start.1
  9.8 1.0 copy-start.2
  10.9 1.0 copy-start.3
  11.9 0.7 copy-start.4
Sparse Core Ops, SparseCore 0:
  101.3 155.5 all-reduce.3

commit v2 on v1

--- a/solution.py
+++ b/solution.py
@@ -1,4 +1,3 @@
-import functools
 import math
 
 import jax
@@ -19,6 +18,7 @@
 PHASE_SCALE = 16.0
 BF = jnp.bfloat16
 F32 = jnp.float32
+MATE = False
 
 
 def real_form(table):
@@ -137,32 +137,40 @@
 
 
 def kernel(
-    off_ref, obj_ref, probe_ref, int_ref, tab_hbm,
-    out_ref, part_ref,
-    region, patch, held, waves, current, gout, gin, rim, rim_in, tab, meas,
-    halo_send, halo_recv, patch_send, patch_recv, grad_send, grad_recv, rim_send, rim_recv, local_sem,
+    off_hbm, obj_hbm, probe_hbm, int_hbm, tab_hbm,
+    out_ref, probe_out,
+    off_ref, obj, region, patch, held, waves, current, gout, gin, relay, rim, rim_in, tab, meas,
+    turned, turned_in, pair, pair_in, spread, spread_in,
+    load_sem, halo_send, halo_recv, patch_send, patch_recv, grad_send, grad_recv, relay_send, relay_recv,
+    rim_send, rim_recv, turned_send, turned_recv, pair_send, pair_recv, spread_send, spread_recv,
 ):
     d = lax.axis_index("depth")
     m = lax.axis_index("scan")
     above, below = lax.rem(m + 31, 32), lax.rem(m + 1, 32)
     core = lax.rem(m, 2)
+    place = m // 2
     x_lo = m // 16
+    mate = m + 1 - 2 * core
     worker = [j * 8 + lax.rem(4 * core + 2 * j + x_lo, 8) for j in range(2)]
     mine = [d == w for w in worker]
     working = jnp.logical_or(mine[0], mine[1])
-
-    tab_copy = pltpu.make_async_copy(tab_hbm, tab, local_sem.at[0])
-    meas_copy = [pltpu.make_async_copy(int_ref.at[j], meas, local_sem.at[1]) for j in range(2)]
-
-    @pl.when(working)
-    def _():
-        tab_copy.start()
+    helping = [d == j * 8 + lax.rem(4 * (1 - core) + 2 * j + x_lo, 8) for j in range(2)]
+
+    off_copy = pltpu.make_async_copy(off_hbm, off_ref, load_sem.at[0])
+    obj_copy = pltpu.make_async_copy(obj_hbm.at[0], obj, load_sem.at[1])
+    tab_copy = pltpu.make_async_copy(tab_hbm, tab, load_sem.at[2])
+    meas_copy = [pltpu.make_async_copy(int_hbm.at[j], meas, load_sem.at[3]) for j in range(2)]
+    probe_copy = pltpu.make_async_copy(probe_hbm, current, load_sem.at[4])
+    obj_copy.start()
+    off_copy.start()
 
     for j in range(2):
 
         @pl.when(mine[j])
         def _():
+            probe_copy.start()
             meas_copy[j].start()
+            tab_copy.start()
 
     barrier = pltpu.get_barrier_semaphore()
     for t in (above, below):
@@ -173,7 +181,12 @@
         def _():
             pl.semaphore_signal(barrier, inc=1, device_id={"depth": worker[j]}, device_id_type=MESH)
 
-    region[1] = obj_ref[0].astype(BF)
+    def greet_place(k, c):
+        @pl.when(k != place)
+        def _():
+            pl.semaphore_signal(barrier, inc=1, device_id={"scan": 2 * k + core}, device_id_type=MESH)
+
+        return c
 
     @pl.when(working)
     def _():
@@ -185,18 +198,26 @@
             return c
 
         lax.fori_loop(0, SLICES, greet, 0)
-        pl.semaphore_wait(barrier, 17)
+
+    lax.fori_loop(0, 16, greet_place, 0)
+    obj_copy.wait()
+    region[1] = obj[...].astype(BF)
+    off_copy.wait()
+    row_off = [off_ref[j, 0] for j in range(2)]
+    col_off = [off_ref[j, 1] for j in range(2)]
+
+    @pl.when(working)
+    def _():
+        pl.semaphore_wait(barrier, 32)
 
     @pl.when(jnp.logical_not(working))
     def _():
-        pl.semaphore_wait(barrier, 4)
+        pl.semaphore_wait(barrier, 19)
 
     down = remote(region.at[1], region.at[0], halo_send.at[0], halo_recv.at[0], "scan", below)
     up = remote(region.at[1], region.at[2], halo_send.at[1], halo_recv.at[1], "scan", above)
     down.start()
     up.start()
-    row_off = [off_ref[j, 0] for j in range(2)]
-    col_off = [off_ref[j, 1] for j in range(2)]
     pick_cols = join(
         *[one_hot((COLS, N), lambda r, c, j=j: r == c + col_off[j]) for j in range(2)], 1
     )
@@ -225,28 +246,42 @@
         def _():
             patch_copy(j).start()
 
-    down.wait_send()
-    up.wait_send()
+    def turned_copy(j, k):
+        rows = pl.ds(pl.multiple_of(k * 16, 16), 16)
+        return remote(turned.at[rows], turned_in.at[j], turned_send.at[k], turned_recv.at[j], "depth", k)
+
+    def turned_keep(j):
+        rows = pl.ds(pl.multiple_of(d * 16, 16), 16)
+        return pltpu.make_async_copy(turned.at[rows], turned_in.at[j], turned_recv.at[j])
+
+    def relay_in(j, s):
+        i = s - 8 * (1 - j)
+        return remote(gout.at[s], relay.at[i], grad_send.at[s], relay_recv.at[i], "scan", mate)
+
+    def relay_out(j, s):
+        i = s - 8 * (1 - j)
+        return pltpu.make_async_remote_copy(
+            src_ref=relay.at[i],
+            dst_ref=gin.at[j],
+            send_sem=relay_send.at[i],
+            recv_sem=grad_recv.at[j],
+            device_id={"depth": s, "scan": mate},
+            device_id_type=MESH,
+        )
 
     def work(j):
+        probe_copy.wait()
+        meas_copy[j].wait()
         tab_copy.wait()
-        meas_copy[j].wait()
-        even_odd = one_hot(
-            (N, N),
-            lambda r, c: c == jnp.where(r < HALF, 2 * r, 2 * r - (N - 1)),
-        )
-        even_odd_t = one_hot(
-            (N, N),
-            lambda r, c: r == jnp.where(c < HALF, 2 * c, 2 * c - (N - 1)),
-        )
+        even_odd = one_hot((N, N), lambda r, c: c == jnp.where(r < HALF, 2 * r, 2 * r - (N - 1)))
+        even_odd_t = one_hot((N, N), lambda r, c: r == jnp.where(c < HALF, 2 * c, 2 * c - (N - 1)))
         measured = meas[...]
         high = measured.astype(BF)
         low = (measured - high.astype(F32)).astype(BF)
         meas[...] = dot(dot(even_odd, high).astype(BF), even_odd_t) + dot(
             dot(even_odd, low).astype(BF), even_odd_t
         )
-        for c in range(2):
-            current[c] = probe_ref[c].astype(BF).astype(F32)
+        current[...] = current[...].astype(BF).astype(F32)
 
         def wait_patch(s):
             @pl.when(s == d)
@@ -290,6 +325,9 @@
         def grad_keep(s):
             return pltpu.make_async_copy(gout.at[s], gin.at[j], grad_recv.at[j])
 
+        def across(s):
+            return jnp.logical_and(MATE, s // 8 != j)
+
         def through(s):
             gr, gi = current[0], current[1]
             wr, wi = waves[s, 0].astype(F32), waves[s, 1].astype(F32)
@@ -300,7 +338,11 @@
             def _():
                 grad_keep(s).start()
 
-            @pl.when(s != d)
+            @pl.when(across(s))
+            def _():
+                relay_in(j, s).start()
+
+            @pl.when(jnp.logical_and(s != d, jnp.logical_not(across(s))))
             def _():
                 grad_copy(s).start()
 
@@ -316,17 +358,25 @@
 
         lax.fori_loop(0, SLICES - 1, backward, 0)
         re, im = through(0)
-        part_ref[0] = re
-        part_ref[1] = im
-
-        def sent(s, carry):
-            @pl.when(s != d)
-            def _():
-                grad_copy(s).wait_send()
+        sums = []
+        for c, part in enumerate((re, im)):
+            chosen = one_hot(
+                (N, 2 * N),
+                lambda r, l, c=c: l
+                == lax.rem(r // 8, 2) * N + (r // 16) * 16 + c * 8 + lax.rem(r, 8),
+            )
+            sums.append(dot(jnp.transpose(part).astype(BF), chosen))
+        turned[...] = (sums[0] + sums[1]).astype(BF)
+        turned_keep(j).start()
+
+        def turn(k, carry):
+            @pl.when(k != d)
+            def _():
+                turned_copy(j, k).start()
 
             return carry
 
-        lax.fori_loop(0, SLICES, sent, 0)
+        lax.fori_loop(0, SLICES, turn, 0)
 
     for j in range(2):
 
@@ -334,15 +384,20 @@
         def _():
             work(j)
 
-    @pl.when(jnp.logical_not(working))
-    def _():
-        part_ref[...] = jnp.zeros_like(part_ref)
+        @pl.when(jnp.logical_and(MATE, helping[j]))
+        def _():
+            def pass_on(i, carry):
+                s = 8 * (1 - j) + 7 - i
+                relay_in(j, s).wait_recv()
+                relay_out(j, s).start()
+                return carry
+
+            lax.fori_loop(0, 8, pass_on, 0)
 
     for j in range(2):
 
         @pl.when(jnp.logical_not(mine[j]))
         def _():
-            patch_copy(j).wait_send()
             remote(gout.at[0], gin.at[j], grad_send.at[0], grad_recv.at[j], "depth", d).wait_recv()
 
         @pl.when(mine[j])
@@ -363,60 +418,170 @@
     to_below = remote(rim.at[1], rim_in.at[1], rim_send.at[1], rim_recv.at[1], "scan", below)
     to_above.start()
     to_below.start()
+
+    for j in range(2):
+
+        @pl.when(mine[j])
+        def _():
+            turned_keep(j).wait()
+
+        @pl.when(jnp.logical_not(mine[j]))
+        def _():
+            turned_copy(j, d).wait_recv()
+
+    both = turned_in[0].astype(F32) + turned_in[1].astype(F32)
+    for h in range(2):
+        pair[h] = both[:, h * N : (h + 1) * N].astype(BF)
+    to_mate = remote(pair.at[1 - core], pair_in, pair_send, pair_recv, "scan", mate)
+    to_mate.start()
+    to_mate.wait_recv()
+    four = pair[core].astype(F32) + pair_in[...].astype(F32)
+    for h in range(2):
+        spread[h] = four[:, h * HALF : (h + 1) * HALF].astype(BF)
+
+    def spread_copy(k):
+        return remote(
+            spread.at[k // 8], spread_in.at[place], spread_send.at[k], spread_recv.at[place], "scan", 2 * k + core
+        )
+
+    def spread_wait(k):
+        return remote(
+            spread.at[k // 8], spread_in.at[k], spread_send.at[k], spread_recv.at[k], "scan", 2 * k + core
+        )
+
+    def send_spread(k, carry):
+        @pl.when(k != place)
+        def _():
+            spread_copy(k).start()
+
+        return carry
+
+    lax.fori_loop(0, 16, send_spread, 0)
+    spread_in[place] = spread[x_lo]
     to_above.wait_recv()
     to_below.wait_recv()
     out_ref[0] = out_ref[0] + rim_in[0].astype(F32) + rim_in[1].astype(F32)
+
+    def take_spread(k, carry):
+        @pl.when(k != place)
+        def _():
+            spread_wait(k).wait_recv()
+
+        return carry
+
+    lax.fori_loop(0, 16, take_spread, 0)
+    everything = spread_in[0].astype(F32)
+    for k in range(1, 16):
+        everything = everything + spread_in[k].astype(F32)
+    own = one_hot((16, HALF), lambda r, l: l == lax.rem(place, 8) * 16 + r)
+    top = everything.astype(BF)
+    rest = (everything - top.astype(F32)).astype(BF)
+    lanes = (((1,), (1,)), ((), ()))
+    final = lax.dot_general(own, top, lanes, preferred_element_type=F32) + lax.dot_general(
+        own, rest, lanes, preferred_element_type=F32
+    )
+    probe_out[0] = final[:8]
+    probe_out[1] = final[8:]
+
+    down.wait_send()
+    up.wait_send()
     to_above.wait_send()
     to_below.wait_send()
+    to_mate.wait_send()
+
+    def sent_spread(k, carry):
+        @pl.when(k != place)
+        def _():
+            spread_copy(k).wait_send()
+
+        return carry
+
+    lax.fori_loop(0, 16, sent_spread, 0)
+    for j in range(2):
+
+        @pl.when(jnp.logical_not(mine[j]))
+        def _():
+            patch_copy(j).wait_send()
+
+        @pl.when(jnp.logical_and(MATE, helping[j]))
+        def _():
+            def passed(i, carry):
+                relay_out(j, 8 * (1 - j) + 7 - i).wait_send()
+                return carry
+
+            lax.fori_loop(0, 8, passed, 0)
+
+        @pl.when(mine[j])
+        def _():
+            def sent(s, carry):
+                @pl.when(s != d)
+                def _():
+                    remote(gout.at[s], gin.at[j], grad_send.at[s], grad_recv.at[j], "depth", s).wait_send()
+                    turned_copy(j, s).wait_send()
+
+                return carry
+
+            lax.fori_loop(0, SLICES, sent, 0)
 
 
 def per_device(tab, object_slices, probe, offsets, intensity):
     vmem = pl.BlockSpec(memory_space=pltpu.VMEM)
+    anywhere = pl.BlockSpec(memory_space=pl.ANY)
     plane = (2, N, N)
-    object_grad, part = pl.pallas_call(
+    strip = (2, TILE, COLS)
+    dma = pltpu.SemaphoreType.DMA
+    return pl.pallas_call(
         kernel,
         out_shape=(
             jax.ShapeDtypeStruct(object_slices.shape, F32),
-            jax.ShapeDtypeStruct(plane, F32),
+            jax.ShapeDtypeStruct((2, 8, 16), F32),
         ),
-        in_specs=[
-            pl.BlockSpec(memory_space=pltpu.SMEM),
-            vmem,
-            vmem,
-            pl.BlockSpec(memory_space=pl.ANY),
-            pl.BlockSpec(memory_space=pl.ANY),
-        ],
+        in_specs=[anywhere] * 5,
         out_specs=(vmem, vmem),
         scratch_shapes=[
-            pltpu.VMEM((3, 2, TILE, COLS), BF),
+            pltpu.SMEM(offsets.shape, jnp.int32),
+            pltpu.VMEM(strip, F32),
+            pltpu.VMEM((3, *strip), BF),
             pltpu.VMEM((2, *plane), BF),
             pltpu.VMEM((SLICES, *plane), BF),
             pltpu.VMEM((SLICES, *plane), BF),
             pltpu.VMEM(plane, F32),
             pltpu.VMEM((SLICES, *plane), BF),
             pltpu.VMEM((2, *plane), BF),
-            pltpu.VMEM((2, 2, TILE, COLS), BF),
-            pltpu.VMEM((2, 2, TILE, COLS), BF),
+            pltpu.VMEM((8, *plane), BF),
+            pltpu.VMEM((2, *strip), BF),
+            pltpu.VMEM((2, *strip), BF),
             pltpu.VMEM((8, 2, N, N), BF),
             pltpu.VMEM((N, N), F32),
-            pltpu.SemaphoreType.DMA((2,)),
-            pltpu.SemaphoreType.DMA((2,)),
-            pltpu.SemaphoreType.DMA((2,)),
-            pltpu.SemaphoreType.DMA((SLICES,)),
-            pltpu.SemaphoreType.DMA((SLICES,)),
-            pltpu.SemaphoreType.DMA((2,)),
-            pltpu.SemaphoreType.DMA((2,)),
-            pltpu.SemaphoreType.DMA((2,)),
-            pltpu.SemaphoreType.DMA((2,)),
+            pltpu.VMEM((N, 2 * N), BF),
+            pltpu.VMEM((2, 16, 2 * N), BF),
+            pltpu.VMEM((2, 16, N), BF),
+            pltpu.VMEM((16, N), BF),
+            pltpu.VMEM((2, 16, HALF), BF),
+            pltpu.VMEM((16, 16, HALF), BF),
+            dma((5,)),
+            dma((2,)),
+            dma((2,)),
+            dma((2,)),
+            dma((SLICES,)),
+            dma((SLICES,)),
+            dma((2,)),
+            dma((8,)),
+            dma((8,)),
+            dma((2,)),
+            dma((2,)),
+            dma((SLICES,)),
+            dma((2,)),
+            dma,
+            dma,
+            dma((16,)),
+            dma((16,)),
         ],
         compiler_params=pltpu.CompilerParams(
-            collective_id=0, has_side_effects=True, vmem_limit_bytes=48 << 20
+            collective_id=0, has_side_effects=True, vmem_limit_bytes=60 << 20
         ),
         name="ptychography_chains",
     )(offsets, object_slices, probe, intensity, tab)
-    partial_sum = lax.psum_scatter(part.astype(BF), "depth", scatter_dimension=2, tiled=True)
-    probe_grad = lax.psum_scatter(partial_sum, "scan", scatter_dimension=1, tiled=True)
-    return object_grad, probe_grad.astype(F32)
 
 
 def solution(mesh):

time: 371 us -> 97.6 us (0.26)
  the two profiles are of different devices: /device:TPU:2 before, /device:TPU:8 now
where the time goes in v2:
time: 97.6 us; the launch traced here: 97.4 us
  Pallas kernels  93.7 us (96%)
  local copies, waits for them, and re-layouts  3.06 us (3%)
    pallas_call x1, Pallas kernels, per_device(): pl.pallas_call(kernel, out_shape=(jax.ShapeDtypeStruct(object_slices.shap...  93.7 us
    unnamed x2, local copies, waits for them, and re-layouts  3.06 us

profile of v2, /device:TPU:8, one launch (start us, length us, event | category | flops | bytes accessed | tf_op | source)
XLA Modules:
  0.0 97.4 jit_solution(12094605544202715810)
XLA Ops:
  0.6 93.7 %ptychography_chains.1 = (f32[1,2,128,384]{3,2,1,0:T(8,128)}, f32[2,8,16]{2,1,0:T(8,128)}) custom-call(s32[2,2]{1,0:T(2,128)} %off_hbm.1, f32[1,2,128,384]{3,2,1,0:T(8,128)} %obj_hbm.1, f32[2,256,256]{2,1,0:T(8,128)} %probe_hbm.1, f32[2,256,256]{2,1,0:T(8,128)} %int_hbm.1, bf16[8,2,256,256]{3,2,1,0:T(8,128)(2,1)} %constant.2.clone.tab_hbm), custom_call_target="tpu_custom_call" | custom-call | tf_op jit(solution)/shard_map/ptychography_chains/pallas_call | solution.py:533
  94.3 1.8 %copy.9 = f32[1,2,128,384]{3,2,1,0:T(8,128)} copy(f32[1,2,128,384]{3,2,1,0:T(8,128)} %get-tuple-element.4) | data formatting | bytes 786432
  96.1 1.3 %copy.10 = f32[2,8,16]{2,1,0:T(8,128)} copy(f32[2,8,16]{2,1,0:T(8,128)} %get-tuple-element.5) | data formatting | bytes 2048

commit v3 on v2

--- a/solution.py
+++ b/solution.py
@@ -18,7 +18,9 @@
 PHASE_SCALE = 16.0
 BF = jnp.bfloat16
 F32 = jnp.float32
-MATE = False
+IN_STEPS = ((1, 7), (1, 7))
+OUT_STEPS = ((), ())
+BENCH = (4, 2, 0, 0)
 
 
 def real_form(table):
@@ -125,6 +127,30 @@
     return join(*butterfly(re, 1), 1), join(*butterfly(im, 1), 1)
 
 
+def keep(hit, x):
+    return jnp.where(hit, x, jnp.zeros_like(x))
+
+
+def rotated_columns(x, off):
+    first, middle, last = x[:, :HALF], x[:, HALF:N], x[:, N:]
+    lane = lax.broadcasted_iota(jnp.int32, first.shape, 1)
+    return join(jnp.where(lane < off, last, first), middle, 1)
+
+
+def object_columns(x, off):
+    first = x[:, :HALF]
+    lane = lax.broadcasted_iota(jnp.int32, first.shape, 1)
+    return jnp.concatenate([keep(lane >= off, first), x[:, HALF:], keep(lane < off, first)], axis=1)
+
+
+def rows_below(shape, off):
+    return lax.broadcasted_iota(jnp.int32, shape, 0) < off
+
+
+def behind(x, off):
+    return lax.rem(x - off + N, N)
+
+
 def remote(src, dst, send, recv, axis, index):
     return pltpu.make_async_remote_copy(
         src_ref=src,
@@ -139,9 +165,9 @@
 def kernel(
     off_hbm, obj_hbm, probe_hbm, int_hbm, tab_hbm,
     out_ref, probe_out,
-    off_ref, obj, region, patch, held, waves, current, gout, gin, relay, rim, rim_in, tab, meas,
+    off_ref, obj, tile, halo, patch, held, waves, current, gout, gin, detour, returned, rim, rim_in, tab, meas,
     turned, turned_in, pair, pair_in, spread, spread_in,
-    load_sem, halo_send, halo_recv, patch_send, patch_recv, grad_send, grad_recv, relay_send, relay_recv,
+    load_sem, halo_send, halo_recv, patch_send, patch_recv, grad_send, grad_recv, detour_send, detour_recv, returned_send, returned_recv,
     rim_send, rim_recv, turned_send, turned_recv, pair_send, pair_recv, spread_send, spread_recv,
 ):
     d = lax.axis_index("depth")
@@ -151,11 +177,31 @@
     place = m // 2
     x_lo = m // 16
     mate = m + 1 - 2 * core
-    worker = [j * 8 + lax.rem(4 * core + 2 * j + x_lo, 8) for j in range(2)]
+    side, z = d // 8, lax.rem(d, 8)
+    bench = [lax.rem(BENCH[0] * core + BENCH[1] * j + BENCH[2] * x_lo + BENCH[3], 8) for j in range(2)]
+    worker = [j * 8 + bench[j] for j in range(2)]
+
+    def steps_in(place_z, j, steps):
+        hit = jnp.bool_(False)
+        for step in steps:
+            hit = jnp.logical_or(hit, place_z == lax.rem(bench[j] + step, 8))
+        return hit
+
+    detoured = [jnp.logical_and(side != j, steps_in(z, j, IN_STEPS[j])) for j in range(2)]
     mine = [d == w for w in worker]
     working = jnp.logical_or(mine[0], mine[1])
-    helping = [d == j * 8 + lax.rem(4 * (1 - core) + 2 * j + x_lo, 8) for j in range(2)]
-
+
+    def either(a, b):
+        return jnp.logical_or(a, b)
+
+    carries = [jnp.logical_and(side == j, steps_in(z, j, IN_STEPS[j])) for j in range(2)]
+    hub = [d == (1 - j) * 8 + bench[j] for j in range(2)]
+    handed = [jnp.logical_and(side != j, steps_in(z, j, OUT_STEPS[j])) for j in range(2)]
+
+    def one(hit):
+        return jnp.where(hit, 1, 0)
+
+    greetings = jnp.where(working, 18, 19) + one(either(*detoured)) + sum(len(OUT_STEPS[j]) * one(hub[j]) for j in range(2))
     off_copy = pltpu.make_async_copy(off_hbm, off_ref, load_sem.at[0])
     obj_copy = pltpu.make_async_copy(obj_hbm.at[0], obj, load_sem.at[1])
     tab_copy = pltpu.make_async_copy(tab_hbm, tab, load_sem.at[2])
@@ -173,25 +219,11 @@
             tab_copy.start()
 
     barrier = pltpu.get_barrier_semaphore()
-    for t in (above, below):
-        pl.semaphore_signal(barrier, inc=1, device_id={"scan": t}, device_id_type=MESH)
-    for j in range(2):
-
-        @pl.when(jnp.logical_not(mine[j]))
-        def _():
-            pl.semaphore_signal(barrier, inc=1, device_id={"depth": worker[j]}, device_id_type=MESH)
-
-    def greet_place(k, c):
-        @pl.when(k != place)
-        def _():
-            pl.semaphore_signal(barrier, inc=1, device_id={"scan": 2 * k + core}, device_id_type=MESH)
-
-        return c
 
     @pl.when(working)
     def _():
         def greet(k, c):
-            @pl.when(jnp.logical_and(k != worker[0], k != worker[1]))
+            @pl.when(k != d)
             def _():
                 pl.semaphore_signal(barrier, inc=1, device_id={"depth": k}, device_id_type=MESH)
 
@@ -199,52 +231,84 @@
 
         lax.fori_loop(0, SLICES, greet, 0)
 
+    for t in (above, below):
+        pl.semaphore_signal(barrier, inc=1, device_id={"scan": t}, device_id_type=MESH)
+    @pl.when(either(*carries))
+    def _():
+        pl.semaphore_signal(barrier, inc=1, device_id={"depth": lax.rem(d + 8, 16)}, device_id_type=MESH)
+
+    for j in range(2):
+
+        @pl.when(handed[j])
+        def _():
+            centre = (1 - j) * 8 + bench[j]
+            pl.semaphore_signal(barrier, inc=1, device_id={"depth": centre}, device_id_type=MESH)
+
+    def greet_place(k, c):
+        @pl.when(k != place)
+        def _():
+            pl.semaphore_signal(barrier, inc=1, device_id={"scan": 2 * k + core}, device_id_type=MESH)
+
+        return c
+
     lax.fori_loop(0, 16, greet_place, 0)
     obj_copy.wait()
-    region[1] = obj[...].astype(BF)
+    tile[...] = obj[...].astype(BF)
     off_copy.wait()
     row_off = [off_ref[j, 0] for j in range(2)]
     col_off = [off_ref[j, 1] for j in range(2)]
 
-    @pl.when(working)
-    def _():
-        pl.semaphore_wait(barrier, 32)
-
-    @pl.when(jnp.logical_not(working))
-    def _():
-        pl.semaphore_wait(barrier, 19)
-
-    down = remote(region.at[1], region.at[0], halo_send.at[0], halo_recv.at[0], "scan", below)
-    up = remote(region.at[1], region.at[2], halo_send.at[1], halo_recv.at[1], "scan", above)
+    pl.semaphore_wait(barrier, greetings)
+
+    down = remote(tile, halo.at[0], halo_send.at[0], halo_recv.at[0], "scan", below)
+    up = remote(tile, halo.at[1], halo_send.at[1], halo_recv.at[1], "scan", above)
     down.start()
     up.start()
-    pick_cols = join(
-        *[one_hot((COLS, N), lambda r, c, j=j: r == c + col_off[j]) for j in range(2)], 1
-    )
-    pick_rows = [one_hot((N, 3 * TILE), lambda r, c, j=j: c == r + row_off[j]) for j in range(2)]
+
+    def patch_copy(j, h):
+        return remote(
+            patch.at[j, h], held.at[d, h], patch_send.at[j, h], patch_recv.at[h, d], "depth", worker[j]
+        )
+
+    def patch_keep(j, h):
+        return pltpu.make_async_copy(patch.at[j, h], held.at[d, h], patch_recv.at[h, d])
+
+    def detour_in(j, h, to):
+        return remote(patch.at[j, h], detour.at[h], patch_send.at[j, h], detour_recv.at[h], "depth", to)
+
+    def detour_out(j, h):
+        source = d + 8 - 16 * j
+        return remote(
+            detour.at[h], held.at[source, h], detour_send.at[h], patch_recv.at[h, source], "depth", worker[j]
+        )
+
+    def hand_in(h):
+        for j in range(2):
+
+            @pl.when(mine[j])
+            def _():
+                patch_keep(j, h).start()
+
+            @pl.when(jnp.logical_not(jnp.logical_or(mine[j], detoured[j])))
+            def _():
+                patch_copy(j, h).start()
+
+            @pl.when(detoured[j])
+            def _():
+                detour_in(j, h, d - 8 + 16 * j).start()
+
+    for j in range(2):
+        for c in range(2):
+            patch[j, 1, c] = rotated_columns(obj[c], col_off[j]).astype(BF)
+    hand_in(1)
     down.wait_recv()
     up.wait_recv()
     for c in range(2):
-        strip = jnp.concatenate([region[t, c] for t in range(3)], axis=0)
-        narrow = dot(strip, pick_cols).astype(BF)
+        over, under = halo[0, c].astype(F32), halo[1, c].astype(F32)
         for j in range(2):
-            patch[j, c] = dot(pick_rows[j], narrow[:, j * N : (j + 1) * N]).astype(BF)
-
-    def patch_copy(j):
-        return remote(patch.at[j], held.at[d], patch_send.at[j], patch_recv.at[d], "depth", worker[j])
-
-    def patch_keep(j):
-        return pltpu.make_async_copy(patch.at[j], held.at[d], patch_recv.at[d])
-
-    for j in range(2):
-
-        @pl.when(mine[j])
-        def _():
-            patch_keep(j).start()
-
-        @pl.when(jnp.logical_not(mine[j]))
-        def _():
-            patch_copy(j).start()
+            rows = jnp.where(rows_below(over.shape, row_off[j]), under, over)
+            patch[j, 0, c] = rotated_columns(rows, col_off[j]).astype(BF)
+    hand_in(0)
 
     def turned_copy(j, k):
         rows = pl.ds(pl.multiple_of(k * 16, 16), 16)
@@ -254,19 +318,23 @@
         rows = pl.ds(pl.multiple_of(d * 16, 16), 16)
         return pltpu.make_async_copy(turned.at[rows], turned_in.at[j], turned_recv.at[j])
 
-    def relay_in(j, s):
-        i = s - 8 * (1 - j)
-        return remote(gout.at[s], relay.at[i], grad_send.at[s], relay_recv.at[i], "scan", mate)
-
-    def relay_out(j, s):
-        i = s - 8 * (1 - j)
-        return pltpu.make_async_remote_copy(
-            src_ref=relay.at[i],
-            dst_ref=gin.at[j],
-            send_sem=relay_send.at[i],
-            recv_sem=grad_recv.at[j],
-            device_id={"depth": s, "scan": mate},
-            device_id_type=MESH,
+    for j in range(2):
+
+        @pl.when(carries[j])
+        def _():
+            for h in (1, 0):
+                detour_in(j, h, d).wait_recv()
+                detour_out(j, h).start()
+
+    def return_in(j, s):
+        i = lax.rem(s, 8)
+        return remote(
+            gout.at[s], returned.at[i], grad_send.at[s], returned_recv.at[i], "depth", (1 - j) * 8 + bench[j]
+        )
+
+    def return_out(j, i):
+        return remote(
+            returned.at[i], gin.at[j], returned_send.at[i], grad_recv.at[j], "depth", (1 - j) * 8 + i
         )
 
     def work(j):
@@ -281,25 +349,33 @@
         meas[...] = dot(dot(even_odd, high).astype(BF), even_odd_t) + dot(
             dot(even_odd, low).astype(BF), even_odd_t
         )
-        current[...] = current[...].astype(BF).astype(F32)
+        turn_rows = one_hot((N, N), lambda r, c: c == behind(r, row_off[j]))
+        turn_cols = one_hot((N, N), lambda r, c: r == behind(c, col_off[j]))
+        for c in range(2):
+            current[c] = dot(dot(turn_rows, current[c].astype(BF)).astype(BF), turn_cols)
 
         def wait_patch(s):
-            @pl.when(s == d)
-            def _():
-                patch_keep(j).wait()
-
-            @pl.when(s != d)
-            def _():
-                remote(
-                    patch.at[j], held.at[s], patch_send.at[j], patch_recv.at[s], "depth", worker[j]
-                ).wait_recv()
+            for h in range(2):
+
+                @pl.when(s == d)
+                def _():
+                    patch_keep(j, h).wait()
+
+                @pl.when(s != d)
+                def _():
+                    remote(
+                        patch.at[j, h], held.at[s, h], patch_send.at[j, h], patch_recv.at[h, s], "depth", worker[j]
+                    ).wait_recv()
+
+        def held_patch(s):
+            return [join(held[s, 0, c], held[s, 1, c], 0).astype(F32) for c in range(2)]
 
         def exit_wave(s):
             wait_patch(s)
             wr, wi = current[0], current[1]
             waves[s, 0] = wr.astype(BF)
             waves[s, 1] = wi.astype(BF)
-            pr, pi = held[s, 0].astype(F32), held[s, 1].astype(F32)
+            pr, pi = held_patch(s)
             return wr * pr - wi * pi, wr * pi + wi * pr
 
         def forward(s, carry):
@@ -326,13 +402,14 @@
             return pltpu.make_async_copy(gout.at[s], gin.at[j], grad_recv.at[j])
 
         def across(s):
-            return jnp.logical_and(MATE, s // 8 != j)
+            return jnp.logical_and(s // 8 != j, steps_in(lax.rem(s, 8), j, OUT_STEPS[j]))
 
         def through(s):
             gr, gi = current[0], current[1]
             wr, wi = waves[s, 0].astype(F32), waves[s, 1].astype(F32)
-            gout[s, 0] = (wr * gr + wi * gi).astype(BF)
-            gout[s, 1] = (wr * gi - wi * gr).astype(BF)
+            for c, product in enumerate((wr * gr + wi * gi, wr * gi - wi * gr)):
+                for h, rows in enumerate(halves(product.astype(BF), 0)):
+                    gout[s, h, c] = rows
 
             @pl.when(s == d)
             def _():
@@ -340,13 +417,13 @@
 
             @pl.when(across(s))
             def _():
-                relay_in(j, s).start()
+                return_in(j, s).start()
 
             @pl.when(jnp.logical_and(s != d, jnp.logical_not(across(s))))
             def _():
                 grad_copy(s).start()
 
-            pr, pi = held[s, 0].astype(F32), held[s, 1].astype(F32)
+            pr, pi = held_patch(s)
             return pr * gr + pi * gi, pr * gi - pi * gr
 
         def backward(i, carry):
@@ -359,13 +436,15 @@
         lax.fori_loop(0, SLICES - 1, backward, 0)
         re, im = through(0)
         sums = []
+        back_cols = one_hot((N, N), lambda r, c: c == behind(r, col_off[j]))
         for c, part in enumerate((re, im)):
-            chosen = one_hot(
-                (N, 2 * N),
-                lambda r, l, c=c: l
-                == lax.rem(r // 8, 2) * N + (r // 16) * 16 + c * 8 + lax.rem(r, 8),
-            )
-            sums.append(dot(jnp.transpose(part).astype(BF), chosen))
+
+            def lane_of(row, c=c):
+                return lax.rem(row // 8, 2) * N + (row // 16) * 16 + c * 8 + lax.rem(row, 8)
+
+            chosen = one_hot((N, 2 * N), lambda r, l: l == lane_of(behind(r, row_off[j])))
+            straight = jnp.transpose(dot(part.astype(BF), back_cols))
+            sums.append(dot(straight.astype(BF), chosen))
         turned[...] = (sums[0] + sums[1]).astype(BF)
         turned_keep(j).start()
 
@@ -384,12 +463,16 @@
         def _():
             work(j)
 
-        @pl.when(jnp.logical_and(MATE, helping[j]))
-        def _():
-            def pass_on(i, carry):
-                s = 8 * (1 - j) + 7 - i
-                relay_in(j, s).wait_recv()
-                relay_out(j, s).start()
+        @pl.when(hub[j])
+        def _():
+            def pass_on(k, carry):
+                i = 7 - k
+
+                @pl.when(steps_in(i, j, OUT_STEPS[j]))
+                def _():
+                    return_in(j, (1 - j) * 8 + i).wait_recv()
+                    return_out(j, i).start()
+
                 return carry
 
             lax.fori_loop(0, 8, pass_on, 0)
@@ -404,16 +487,17 @@
         def _():
             pltpu.make_async_copy(gout.at[d], gin.at[j], grad_recv.at[j]).wait()
 
-    put_cols = [one_hot((N, COLS), lambda r, c, j=j: c == r + col_off[j]) for j in range(2)]
-    put_rows = join(
-        *[one_hot((3 * TILE, N), lambda r, c, j=j: r == c + row_off[j]) for j in range(2)], 1
-    )
     for c in range(2):
-        wide = join(*[dot(gin[j, c], put_cols[j]).astype(BF) for j in range(2)], 0)
-        total = dot(put_rows, wide)
-        rim[0, c] = total[:TILE].astype(BF)
-        rim[1, c] = total[2 * TILE :].astype(BF)
-        out_ref[0, c] = total[TILE : 2 * TILE]
+        own, over, under = 0.0, 0.0, 0.0
+        for j in range(2):
+            own = own + object_columns(gin[j, 1, c].astype(F32), col_off[j])
+            edge = object_columns(gin[j, 0, c].astype(F32), col_off[j])
+            low = rows_below(edge.shape, row_off[j])
+            over = over + keep(jnp.logical_not(low), edge)
+            under = under + keep(low, edge)
+        out_ref[0, c] = own
+        rim[0, c] = over.astype(BF)
+        rim[1, c] = under.astype(BF)
     to_above = remote(rim.at[0], rim_in.at[0], rim_send.at[0], rim_recv.at[0], "scan", above)
     to_below = remote(rim.at[1], rim_in.at[1], rim_send.at[1], rim_recv.at[1], "scan", below)
     to_above.start()
@@ -501,12 +585,21 @@
 
         @pl.when(jnp.logical_not(mine[j]))
         def _():
-            patch_copy(j).wait_send()
-
-        @pl.when(jnp.logical_and(MATE, helping[j]))
+            patch_copy(j, 0).wait_send()
+            patch_copy(j, 1).wait_send()
+
+        @pl.when(carries[j])
+        def _():
+            for h in range(2):
+                detour_out(j, h).wait_send()
+
+        @pl.when(hub[j])
         def _():
             def passed(i, carry):
-                relay_out(j, 8 * (1 - j) + 7 - i).wait_send()
+                @pl.when(steps_in(i, j, OUT_STEPS[j]))
+                def _():
+                    return_out(j, i).wait_send()
+
                 return carry
 
             lax.fori_loop(0, 8, passed, 0)
@@ -524,31 +617,40 @@
             lax.fori_loop(0, SLICES, sent, 0)
 
 
+def results(grad_ref, probe_ref, out_ref, probe_out):
+    out_ref[...] = grad_ref[...]
+    probe_out[...] = probe_ref[...]
+
+
 def per_device(tab, object_slices, probe, offsets, intensity):
     vmem = pl.BlockSpec(memory_space=pltpu.VMEM)
     anywhere = pl.BlockSpec(memory_space=pl.ANY)
     plane = (2, N, N)
     strip = (2, TILE, COLS)
+    parts = (2, 2, HALF, N)
     dma = pltpu.SemaphoreType.DMA
-    return pl.pallas_call(
+    outs = (
+        jax.ShapeDtypeStruct(object_slices.shape, F32),
+        jax.ShapeDtypeStruct((2, 8, 16), F32),
+    )
+    grads = pl.pallas_call(
         kernel,
-        out_shape=(
-            jax.ShapeDtypeStruct(object_slices.shape, F32),
-            jax.ShapeDtypeStruct((2, 8, 16), F32),
-        ),
+        out_shape=outs,
         in_specs=[anywhere] * 5,
         out_specs=(vmem, vmem),
         scratch_shapes=[
             pltpu.SMEM(offsets.shape, jnp.int32),
             pltpu.VMEM(strip, F32),
-            pltpu.VMEM((3, *strip), BF),
-            pltpu.VMEM((2, *plane), BF),
-            pltpu.VMEM((SLICES, *plane), BF),
+            pltpu.VMEM(strip, BF),
+            pltpu.VMEM((2, *strip), BF),
+            pltpu.VMEM((2, *parts), BF),
+            pltpu.VMEM((SLICES, *parts), BF),
             pltpu.VMEM((SLICES, *plane), BF),
             pltpu.VMEM(plane, F32),
-            pltpu.VMEM((SLICES, *plane), BF),
-            pltpu.VMEM((2, *plane), BF),
-            pltpu.VMEM((8, *plane), BF),
+            pltpu.VMEM((SLICES, *parts), BF),
+            pltpu.VMEM((2, *parts), BF),
+            pltpu.VMEM(parts, BF),
+            pltpu.VMEM((8, *parts), BF),
             pltpu.VMEM((2, *strip), BF),
             pltpu.VMEM((2, *strip), BF),
             pltpu.VMEM((8, 2, N, N), BF),
@@ -562,9 +664,11 @@
             dma((5,)),
             dma((2,)),
             dma((2,)),
+            dma((2, 2)),
+            dma((2, SLICES)),
+            dma((SLICES,)),
             dma((2,)),
-            dma((SLICES,)),
-            dma((SLICES,)),
+            dma((2,)),
             dma((2,)),
             dma((8,)),
             dma((8,)),
@@ -582,6 +686,13 @@
         ),
         name="ptychography_chains",
     )(offsets, object_slices, probe, intensity, tab)
+    return pl.pallas_call(
+        results,
+        out_shape=outs,
+        in_specs=[vmem] * 2,
+        out_specs=(vmem, vmem),
+        name="results",
+    )(*grads)
 
 
 def solution(mesh):

time: 97.6 us -> 85.4 us (0.88)
  the two profiles are of different devices: /device:TPU:8 before, /device:TPU:1 now
where the time goes in v3:
time: 85.4 us; the launch traced here: 85.3 us
  Pallas kernels  84.6 us (99%)
    pallas_call x1, Pallas kernels, per_device(): pl.pallas_call(kernel, out_shape=outs, in_specs=[anywhere] * 5, out_specs...  82.9 us
    pallas_call x1, Pallas kernels, per_device(): pl.pallas_call(results, out_shape=outs, in_specs=[vmem] * 2, out_specs=(v...  1.77 us

profile of v3, /device:TPU:1, one launch (start us, length us, event | category | flops | bytes accessed | tf_op | source)
XLA Modules:
  0.0 85.3 jit_solution(6624210539493675988)
XLA Ops:
  0.6 82.9 %ptychography_chains.1 = (f32[1,2,128,384]{3,2,1,0:T(8,128)}, f32[2,8,16]{2,1,0:T(8,128)}) custom-call(s32[2,2]{1,0:T(2,128)} %off_hbm.1, f32[1,2,128,384]{3,2,1,0:T(8,128)} %obj_hbm.1, f32[2,256,256]{2,1,0:T(8,128)} %probe_hbm.1, f32[2,256,256]{2,1,0:T(8,128)} %int_hbm.1, bf16[8,2,256,256]{3,2,1,0:T(8,128)(2,1)} %constant.2.clone.tab_hbm), custom_call_target="tpu_custom_call" | custom-call | tf_op jit(solution)/shard_map/ptychography_chains/pallas_call | solution.py:636
  83.5 1.8 %results.1 = (f32[1,2,128,384]{3,2,1,0:T(8,128)}, f32[2,8,16]{2,1,0:T(8,128)}) custom-call(f32[1,2,128,384]{3,2,1,0:T(8,128)} %get-tuple-element.4.grad_ref, f32[2,8,16]{2,1,0:T(8,128)} %get-tuple-element.5.probe_ref), custom_call_target="tpu_custom_call" | custom-call | tf_op jit(solution)/shard_map/results/pallas_call | solution.py:689

commit v4 on v3

--- a/solution.py
+++ b/solution.py
@@ -18,9 +18,10 @@
 PHASE_SCALE = 16.0
 BF = jnp.bfloat16
 F32 = jnp.float32
-IN_STEPS = ((1, 7), (1, 7))
+IN_STEPS = ((), (1, 7))
 OUT_STEPS = ((), ())
-BENCH = (4, 2, 0, 0)
+LATE = (4, 8)
+BENCH = (4, 2, 0)
 
 
 def real_form(table):
@@ -166,19 +167,18 @@
     off_hbm, obj_hbm, probe_hbm, int_hbm, tab_hbm,
     out_ref, probe_out,
     off_ref, obj, tile, halo, patch, held, waves, current, gout, gin, detour, returned, rim, rim_in, tab, meas,
-    turned, turned_in, pair, pair_in, spread, spread_in,
+    blocks, gathered, turned, turned_in, pair, pair_in,
     load_sem, halo_send, halo_recv, patch_send, patch_recv, grad_send, grad_recv, detour_send, detour_recv, returned_send, returned_recv,
-    rim_send, rim_recv, turned_send, turned_recv, pair_send, pair_recv, spread_send, spread_recv,
+    rim_send, rim_recv, block_send, block_recv, turned_send, turned_recv, pair_send, pair_recv,
 ):
     d = lax.axis_index("depth")
     m = lax.axis_index("scan")
     above, below = lax.rem(m + 31, 32), lax.rem(m + 1, 32)
     core = lax.rem(m, 2)
     place = m // 2
-    x_lo = m // 16
     mate = m + 1 - 2 * core
     side, z = d // 8, lax.rem(d, 8)
-    bench = [lax.rem(BENCH[0] * core + BENCH[1] * j + BENCH[2] * x_lo + BENCH[3], 8) for j in range(2)]
+    bench = [lax.rem(BENCH[0] * core + BENCH[1] * j + BENCH[2], 8) for j in range(2)]
     worker = [j * 8 + bench[j] for j in range(2)]
 
     def steps_in(place_z, j, steps):
@@ -201,7 +201,7 @@
     def one(hit):
         return jnp.where(hit, 1, 0)
 
-    greetings = jnp.where(working, 18, 19) + one(either(*detoured)) + sum(len(OUT_STEPS[j]) * one(hub[j]) for j in range(2))
+    greetings = jnp.where(working, 18, 4) + one(either(*detoured)) + sum(len(OUT_STEPS[j]) * one(hub[j]) for j in range(2))
     off_copy = pltpu.make_async_copy(off_hbm, off_ref, load_sem.at[0])
     obj_copy = pltpu.make_async_copy(obj_hbm.at[0], obj, load_sem.at[1])
     tab_copy = pltpu.make_async_copy(tab_hbm, tab, load_sem.at[2])
@@ -251,7 +251,10 @@
 
         return c
 
-    lax.fori_loop(0, 16, greet_place, 0)
+    @pl.when(working)
+    def _():
+        lax.fori_loop(0, 16, greet_place, 0)
+
     obj_copy.wait()
     tile[...] = obj[...].astype(BF)
     off_copy.wait()
@@ -309,6 +312,16 @@
             rows = jnp.where(rows_below(over.shape, row_off[j]), under, over)
             patch[j, 0, c] = rotated_columns(rows, col_off[j]).astype(BF)
     hand_in(0)
+
+    def block_copy(k):
+        return remote(
+            blocks.at[k], gathered.at[place], block_send.at[k], block_recv.at[place], "scan", 2 * k + core
+        )
+
+    def block_wait(k):
+        return remote(
+            blocks.at[k], gathered.at[k], block_send.at[k], block_recv.at[k], "scan", 2 * k + core
+        )
 
     def turned_copy(j, k):
         rows = pl.ds(pl.multiple_of(k * 16, 16), 16)
@@ -404,6 +417,19 @@
         def across(s):
             return jnp.logical_and(s // 8 != j, steps_in(lax.rem(s, 8), j, OUT_STEPS[j]))
 
+        def send_grad(s):
+            @pl.when(s == d)
+            def _():
+                grad_keep(s).start()
+
+            @pl.when(across(s))
+            def _():
+                return_in(j, s).start()
+
+            @pl.when(jnp.logical_and(s != d, jnp.logical_not(across(s))))
+            def _():
+                grad_copy(s).start()
+
         def through(s):
             gr, gi = current[0], current[1]
             wr, wi = waves[s, 0].astype(F32), waves[s, 1].astype(F32)
@@ -411,17 +437,9 @@
                 for h, rows in enumerate(halves(product.astype(BF), 0)):
                     gout[s, h, c] = rows
 
-            @pl.when(s == d)
-            def _():
-                grad_keep(s).start()
-
-            @pl.when(across(s))
-            def _():
-                return_in(j, s).start()
-
-            @pl.when(jnp.logical_and(s != d, jnp.logical_not(across(s))))
-            def _():
-                grad_copy(s).start()
+            @pl.when(jnp.logical_or(s < LATE[0], s >= LATE[1]))
+            def _():
+                send_grad(s)
 
             pr, pi = held_patch(s)
             return pr * gr + pi * gi, pr * gi - pi * gr
@@ -435,17 +453,36 @@
 
         lax.fori_loop(0, SLICES - 1, backward, 0)
         re, im = through(0)
-        sums = []
+        back_rows = one_hot((N, N), lambda r, c: r == behind(c, row_off[j]))
         back_cols = one_hot((N, N), lambda r, c: c == behind(r, col_off[j]))
         for c, part in enumerate((re, im)):
-
-            def lane_of(row, c=c):
-                return lax.rem(row // 8, 2) * N + (row // 16) * 16 + c * 8 + lax.rem(row, 8)
-
-            chosen = one_hot((N, 2 * N), lambda r, l: l == lane_of(behind(r, row_off[j])))
-            straight = jnp.transpose(dot(part.astype(BF), back_cols))
-            sums.append(dot(straight.astype(BF), chosen))
-        turned[...] = (sums[0] + sums[1]).astype(BF)
+            straight = dot(dot(back_rows, part.astype(BF)).astype(BF), back_cols).astype(BF)
+            for k in range(16):
+                blocks[k, c] = straight[16 * k : 16 * k + 16]
+
+        def send_block(k, carry):
+            @pl.when(k != place)
+            def _():
+                block_copy(k).start()
+
+            return carry
+
+        lax.fori_loop(0, 16, send_block, 0)
+        gathered[place] = blocks[place]
+
+        def take_block(k, carry):
+            @pl.when(k != place)
+            def _():
+                block_wait(k).wait_recv()
+
+            return carry
+
+        lax.fori_loop(0, 16, take_block, 0)
+        total = gathered[0].astype(F32)
+        for k in range(1, 16):
+            total = total + gathered[k].astype(F32)
+        tall = jnp.concatenate([total[0], total[1], jnp.zeros((HALF - 32, N), F32)], axis=0)
+        turned[...] = jnp.transpose(tall).astype(BF)
         turned_keep(j).start()
 
         def turn(k, carry):
@@ -457,6 +494,12 @@
 
         lax.fori_loop(0, SLICES, turn, 0)
 
+        def send_late(i, carry):
+            send_grad(LATE[1] - 1 - i)
+            return carry
+
+        lax.fori_loop(0, LATE[1] - LATE[0], send_late, 0)
+
     for j in range(2):
 
         @pl.when(mine[j])
@@ -466,7 +509,7 @@
         @pl.when(hub[j])
         def _():
             def pass_on(k, carry):
-                i = 7 - k
+                i = 7 - k if j == 0 else lax.rem(LATE[0] + 7 - k, 8)
 
                 @pl.when(steps_in(i, j, OUT_STEPS[j]))
                 def _():
@@ -514,50 +557,16 @@
             turned_copy(j, d).wait_recv()
 
     both = turned_in[0].astype(F32) + turned_in[1].astype(F32)
-    for h in range(2):
-        pair[h] = both[:, h * N : (h + 1) * N].astype(BF)
-    to_mate = remote(pair.at[1 - core], pair_in, pair_send, pair_recv, "scan", mate)
+    pair[...] = both.astype(BF)
+    to_mate = remote(pair, pair_in, pair_send, pair_recv, "scan", mate)
     to_mate.start()
-    to_mate.wait_recv()
-    four = pair[core].astype(F32) + pair_in[...].astype(F32)
-    for h in range(2):
-        spread[h] = four[:, h * HALF : (h + 1) * HALF].astype(BF)
-
-    def spread_copy(k):
-        return remote(
-            spread.at[k // 8], spread_in.at[place], spread_send.at[k], spread_recv.at[place], "scan", 2 * k + core
-        )
-
-    def spread_wait(k):
-        return remote(
-            spread.at[k // 8], spread_in.at[k], spread_send.at[k], spread_recv.at[k], "scan", 2 * k + core
-        )
-
-    def send_spread(k, carry):
-        @pl.when(k != place)
-        def _():
-            spread_copy(k).start()
-
-        return carry
-
-    lax.fori_loop(0, 16, send_spread, 0)
-    spread_in[place] = spread[x_lo]
     to_above.wait_recv()
     to_below.wait_recv()
     out_ref[0] = out_ref[0] + rim_in[0].astype(F32) + rim_in[1].astype(F32)
 
-    def take_spread(k, carry):
-        @pl.when(k != place)
-        def _():
-            spread_wait(k).wait_recv()
-
-        return carry
-
-    lax.fori_loop(0, 16, take_spread, 0)
-    everything = spread_in[0].astype(F32)
-    for k in range(1, 16):
-        everything = everything + spread_in[k].astype(F32)
-    own = one_hot((16, HALF), lambda r, l: l == lax.rem(place, 8) * 16 + r)
+    to_mate.wait_recv()
+    everything = both + pair_in[...].astype(F32)
+    own = one_hot((16, HALF), lambda r, l: l == (r // 8) * 16 + core * 8 + lax.rem(r, 8))
     top = everything.astype(BF)
     rest = (everything - top.astype(F32)).astype(BF)
     lanes = (((1,), (1,)), ((), ()))
@@ -573,14 +582,6 @@
     to_below.wait_send()
     to_mate.wait_send()
 
-    def sent_spread(k, carry):
-        @pl.when(k != place)
-        def _():
-            spread_copy(k).wait_send()
-
-        return carry
-
-    lax.fori_loop(0, 16, sent_spread, 0)
     for j in range(2):
 
         @pl.when(jnp.logical_not(mine[j]))
@@ -611,6 +612,10 @@
                 def _():
                     remote(gout.at[s], gin.at[j], grad_send.at[s], grad_recv.at[j], "depth", s).wait_send()
                     turned_copy(j, s).wait_send()
+
+                @pl.when(s != place)
+                def _():
+                    block_copy(s).wait_send()
 
                 return carry
 
@@ -655,12 +660,12 @@
             pltpu.VMEM((2, *strip), BF),
             pltpu.VMEM((8, 2, N, N), BF),
             pltpu.VMEM((N, N), F32),
-            pltpu.VMEM((N, 2 * N), BF),
-            pltpu.VMEM((2, 16, 2 * N), BF),
-            pltpu.VMEM((2, 16, N), BF),
-            pltpu.VMEM((16, N), BF),
+            pltpu.VMEM((16, 2, 16, N), BF),
+            pltpu.VMEM((16, 2, 16, N), BF),
+            pltpu.VMEM((N, HALF), BF),
             pltpu.VMEM((2, 16, HALF), BF),
-            pltpu.VMEM((16, 16, HALF), BF),
+            pltpu.VMEM((16, HALF), BF),
+            pltpu.VMEM((16, HALF), BF),
             dma((5,)),
             dma((2,)),
             dma((2,)),
@@ -674,12 +679,12 @@
             dma((8,)),
             dma((2,)),
             dma((2,)),
+            dma((16,)),
+            dma((16,)),
             dma((SLICES,)),
             dma((2,)),
             dma,
             dma,
-            dma((16,)),
-            dma((16,)),
         ],
         compiler_params=pltpu.CompilerParams(
             collective_id=0, has_side_effects=True, vmem_limit_bytes=60 << 20

time: 85.4 us -> 78.4 us (0.918)
  the two profiles are of different devices: /device:TPU:1 before, /device:TPU:2 now
where the time goes in v4:
time: 78.4 us; the launch traced here: 78.3 us
  Pallas kernels  77.6 us (99%)
    pallas_call x1, Pallas kernels, per_device(): pl.pallas_call(kernel, out_shape=outs, in_specs=[anywhere] * 5, out_specs...  75.9 us
    pallas_call x1, Pallas kernels, per_device(): pl.pallas_call(results, out_shape=outs, in_specs=[vmem] * 2, out_specs=(v...  1.77 us

profile of v4, /device:TPU:2, one launch (start us, length us, event | category | flops | bytes accessed | tf_op | source)
XLA Modules:
  0.0 78.3 jit_solution(6635098861239657565)
XLA Ops:
  0.6 75.9 %ptychography_chains.1 = (f32[1,2,128,384]{3,2,1,0:T(8,128)}, f32[2,8,16]{2,1,0:T(8,128)}) custom-call(s32[2,2]{1,0:T(2,128)} %off_hbm.1, f32[1,2,128,384]{3,2,1,0:T(8,128)} %obj_hbm.1, f32[2,256,256]{2,1,0:T(8,128)} %probe_hbm.1, f32[2,256,256]{2,1,0:T(8,128)} %int_hbm.1, bf16[8,2,256,256]{3,2,1,0:T(8,128)(2,1)} %constant.2.clone.tab_hbm), custom_call_target="tpu_custom_call" | custom-call | tf_op jit(solution)/shard_map/ptychography_chains/pallas_call | solution.py:641
  76.5 1.8 %results.1 = (f32[1,2,128,384]{3,2,1,0:T(8,128)}, f32[2,8,16]{2,1,0:T(8,128)}) custom-call(f32[1,2,128,384]{3,2,1,0:T(8,128)} %get-tuple-element.4.grad_ref, f32[2,8,16]{2,1,0:T(8,128)} %get-tuple-element.5.probe_ref), custom_call_target="tpu_custom_call" | custom-call | tf_op jit(solution)/shard_map/results/pallas_call | solution.py:694

commit v5 on v4

--- a/solution.py
+++ b/solution.py
@@ -20,7 +20,7 @@
 F32 = jnp.float32
 IN_STEPS = ((), (1, 7))
 OUT_STEPS = ((), ())
-LATE = (4, 8)
+LATE = (5, 8)
 BENCH = (4, 2, 0)
 
 
@@ -428,7 +428,10 @@
 
             @pl.when(jnp.logical_and(s != d, jnp.logical_not(across(s))))
             def _():
-                grad_copy(s).start()
+                for h in range(2):
+                    remote(
+                        gout.at[s, h], gin.at[j, h], grad_send.at[s], grad_recv.at[j], "depth", s
+                    ).start()
 
         def through(s):
             gr, gi = current[0], current[1]
@@ -495,7 +498,7 @@
         lax.fori_loop(0, SLICES, turn, 0)
 
         def send_late(i, carry):
-            send_grad(LATE[1] - 1 - i)
+            send_grad(LATE[0] + i)
             return carry
 
         lax.fori_loop(0, LATE[1] - LATE[0], send_late, 0)

time: 78.4 us -> 78.4 us (level)
  no operation moved by 1% of the time
where the time goes in v5:
time: 78.4 us; the launch traced here: 78.3 us
  Pallas kernels  77.7 us (99%)
    pallas_call x1, Pallas kernels, per_device(): pl.pallas_call(kernel, out_shape=outs, in_specs=[anywhere] * 5, out_specs...  75.9 us
    pallas_call x1, Pallas kernels, per_device(): pl.pallas_call(results, out_shape=outs, in_specs=[vmem] * 2, out_specs=(v...  1.77 us

profile of v5, /device:TPU:2, one launch (start us, length us, event | category | flops | bytes accessed | tf_op | source)
XLA Modules:
  0.0 78.3 jit_solution(13215303218758413331)
XLA Ops:
  0.6 75.9 %ptychography_chains.1 = (f32[1,2,128,384]{3,2,1,0:T(8,128)}, f32[2,8,16]{2,1,0:T(8,128)}) custom-call(s32[2,2]{1,0:T(2,128)} %off_hbm.1, f32[1,2,128,384]{3,2,1,0:T(8,128)} %obj_hbm.1, f32[2,256,256]{2,1,0:T(8,128)} %probe_hbm.1, f32[2,256,256]{2,1,0:T(8,128)} %int_hbm.1, bf16[8,2,256,256]{3,2,1,0:T(8,128)(2,1)} %constant.2.clone.tab_hbm), custom_call_target="tpu_custom_call" | custom-call | tf_op jit(solution)/shard_map/ptychography_chains/pallas_call | solution.py:644
  76.5 1.8 %results.1 = (f32[1,2,128,384]{3,2,1,0:T(8,128)}, f32[2,8,16]{2,1,0:T(8,128)}) custom-call(f32[1,2,128,384]{3,2,1,0:T(8,128)} %get-tuple-element.4.grad_ref, f32[2,8,16]{2,1,0:T(8,128)} %get-tuple-element.5.probe_ref), custom_call_target="tpu_custom_call" | custom-call | tf_op jit(solution)/shard_map/results/pallas_call | solution.py:697
